TPU v7x, 256 devices: a whole 4x4x8 slice. The times are simulated.
256 devices in a mesh: grp: 8 (over z_lo, core), dp: 32 (over z_hi, y, x).
Axes of the slice: x: 4, y: 4, z: 8 (z_hi: 2, z_lo: 4; z = z_hi * 4 + z_lo), core: 2. Of those that a mesh axis runs over, the one named last changes fastest.
Arguments:
- patches: bfloat16 [262144, 1152], P(('grp', 'dp')), may hold values from -180 to 180
- patch_counts: int32 [1024], P(('grp', 'dp')), may hold values from 64 to 256, as said below
- pack_offsets: int32 [1024], P(('grp', 'dp')), may hold values from 0 to 960, as said below
- norm_gain: float32 [1152], replicated, may hold values from 0.1 to 1.9
- mlp_in: bfloat16 [1152, 4304], P('dp'), may hold values from -0.1875 to 0.1875
- mlp_out: bfloat16 [4304, 1152], P(None, 'dp'), may hold values from -0.09375 to 0.09375
- probe_query: bfloat16 [1152], replicated, may hold values from -4 to 4
- key_weight: bfloat16 [1152, 1152], replicated, may hold values from -0.1875 to 0.1875
- value_weight: bfloat16 [1152, 1152], replicated, may hold values from -0.1875 to 0.1875
- out_weight: bfloat16 [1152, 1152], replicated, may hold values from -0.1875 to 0.1875
- text_embed: bfloat16 [1024, 1152], P(('grp', 'dp')), may hold values from -6 to 6
- pair_label: int32 [1024], replicated, may hold values from 0 to 511
- logit_scale: float32 [1], replicated, may hold values from 4 to 16
- logit_bias: float32 [1], replicated, may hold values from -4 to -1
Outputs:
- loss: float32 [], replicated
- image_grad: float32 [1024, 1152], P(('grp', 'dp'))
- text_grad: float32 [1024, 1152], P(('grp', 'dp'))
Inputs may be any that keep to these rules, and one draw needn't show every extreme that they name: `patch_counts`: the counts of the 4 images of one device sum to 512. `pack_offsets`: the images held in one pack occupy disjoint rows that end by row 1024; in every group some pack is filled completely.
All inputs are finite; a program needn't handle non-finite values.
Results may differ from a plain program's by a relative error of at most 0.008.
The roundings to bfloat16 on the way count: a program that leaves them out, or rounds other values in their place, can miss the bound.
Values may be sent and summed in bfloat16 or wider, within the bound.
A program may use at most 128 MiB of HBM per device.

v0:
```python
import math

import jax
import jax.numpy as jnp
from jax import lax
from jax.sharding import PartitionSpec as P

HEAD_DIM = 72
SLOT = 256


EPSILON = 1e-06


def from_behind(value, axis, by):
    devices = lax.axis_size(axis)
    return lax.ppermute(value, axis, [(i, (i + by) % devices) for i in range(devices)])


def feed_forward(patch_rows, norm_gain, mlp_in, mlp_out):
    widened = patch_rows.astype(jnp.float32)
    center = jnp.mean(widened, axis=1, keepdims=True)
    spread = jnp.mean(jnp.square(widened - center), axis=1, keepdims=True)
    normed = ((widened - center) * lax.rsqrt(spread + EPSILON) * norm_gain).astype(jnp.bfloat16)
    hidden = jnp.dot(
        normed, lax.all_gather(mlp_in, "dp", axis=0, tiled=True), preferred_element_type=jnp.float32
    )
    active = jax.nn.gelu(hidden, approximate=True).astype(jnp.bfloat16)
    mixed = jnp.dot(
        active,
        lax.all_gather(mlp_out, "dp", axis=1, tiled=True),
        preferred_element_type=jnp.float32,
    )
    return (widened + mixed).astype(jnp.bfloat16)


def head_keys(key_weight, probe_query):
    model_width = key_weight.shape[0]
    head_count = model_width // HEAD_DIM
    head_of_row = jnp.arange(model_width) // HEAD_DIM
    probe_block = jnp.where(
        head_of_row[:, None] == jnp.arange(head_count)[None, :],
        probe_query[:, None],
        jnp.zeros((), probe_query.dtype),
    )
    return (
        jnp.dot(key_weight, probe_block, preferred_element_type=jnp.float32) / math.sqrt(HEAD_DIM)
    ).astype(jnp.bfloat16)


def attend(states, member, head_key, value_weight, out_weight):
    row_count, model_width = states.shape
    image_count = member.shape[1]
    head_count = head_key.shape[1]
    scores = jnp.dot(states, head_key, preferred_element_type=jnp.float32)
    masked = jnp.where(member[:, :, None], scores[:, None, :], -1e30)
    highest = jnp.max(masked, axis=0)
    raised = jnp.exp(masked - highest[None])
    denominator = jnp.sum(raised, axis=0)
    weights_low = (
        (raised / denominator[None])
        .astype(jnp.bfloat16)
        .reshape(row_count, image_count * head_count)
    )
    mean_states = lax.dot_general(
        weights_low, states, (((0,), (0,)), ((), ())), preferred_element_type=jnp.float32
    ).astype(jnp.bfloat16)
    per_head = mean_states.reshape(image_count, head_count, model_width)
    head_values = jnp.einsum(
        "khd,dhe->khe",
        per_head,
        value_weight.reshape(model_width, head_count, HEAD_DIM),
        preferred_element_type=jnp.float32,
    )
    mixed = head_values.astype(jnp.bfloat16).reshape(image_count, model_width)
    return jnp.dot(mixed, out_weight, preferred_element_type=jnp.float32)


def per_device(
    patches,
    patch_counts,
    pack_offsets,
    norm_gain,
    mlp_in,
    mlp_out,
    probe_query,
    key_weight,
    value_weight,
    out_weight,
    text_embed,
    pair_label,
    logit_scale,
    logit_bias,
):
    images = patch_counts.shape[0]
    stride = lax.axis_size("dp") // images
    head_key = head_keys(key_weight, probe_query)
    slot_index = jnp.arange(images, dtype=jnp.int32)
    windows = []
    for ordinal in range(images):
        picked = jnp.clip(
            pack_offsets[ordinal] + jnp.arange(SLOT, dtype=jnp.int32), 0, patches.shape[0] - 1
        )
        window = jnp.take(patches, picked, axis=0)
        if ordinal > 0:
            window = from_behind(window, "dp", -ordinal * stride)
        windows.append(window)
    stacked = jnp.concatenate(windows, axis=0)
    bounds_end = jnp.cumsum(patch_counts)
    starts = bounds_end - patch_counts
    row_index = jnp.arange(2 * SLOT, dtype=jnp.int32)
    segment = jnp.sum((row_index[:, None] >= bounds_end[None, :]).astype(jnp.int32), axis=1)
    source = segment * SLOT + row_index - starts[segment]
    gathered = jnp.take(stacked, source, axis=0)
    states = feed_forward(gathered, norm_gain, mlp_in, mlp_out)
    pooled = attend(
        states, segment[:, None] == slot_index[None, :], head_key, value_weight, out_weight
    )
    logit_mult = logit_scale[0]
    logit_shift = logit_bias[0]
    image_inv = lax.rsqrt(jnp.sum(pooled * pooled, axis=1, keepdims=True) + EPSILON)
    image_unit = pooled * image_inv
    image_low = image_unit.astype(jnp.bfloat16)
    text_wide = text_embed.astype(jnp.float32)
    text_inv = lax.rsqrt(jnp.sum(text_wide * text_wide, axis=1, keepdims=True) + EPSILON)
    text_unit = text_wide * text_inv
    text_low = text_unit.astype(jnp.bfloat16)
    text_all = lax.all_gather(text_low, ("grp", "dp"), axis=0, tiled=True)
    own_start = lax.axis_index(("grp", "dp")) * images
    own_labels = lax.dynamic_slice_in_dim(pair_label, own_start, images)
    logits = (
        logit_mult
        * lax.dot_general(
            image_low, text_all, (((1,), (1,)), ((), ())), preferred_element_type=jnp.float32
        )
        + logit_shift
    )
    target_sign = jnp.where(own_labels[:, None] == pair_label[None, :], 1.0, -1.0).astype(
        jnp.float32
    )
    partial_loss = jnp.sum(-jax.nn.log_sigmoid(target_sign * logits))
    slope_low = (logit_mult * -target_sign * jax.nn.sigmoid(-target_sign * logits)).astype(
        jnp.bfloat16
    )
    image_push = jnp.dot(slope_low, text_all, preferred_element_type=jnp.float32)
    image_grad = (
        image_push - image_unit * jnp.sum(image_unit * image_push, axis=1, keepdims=True)
    ) * image_inv
    text_push = lax.psum_scatter(
        lax.dot_general(
            slope_low, image_low, (((0,), (0,)), ((), ())), preferred_element_type=jnp.float32
        ),
        ("grp", "dp"),
        scatter_dimension=0,
        tiled=True,
    )
    text_grad = (
        text_push - text_unit * jnp.sum(text_unit * text_push, axis=1, keepdims=True)
    ) * text_inv
    loss_value = lax.psum(partial_loss, ("grp", "dp")) / text_all.shape[0]
    return (loss_value, image_grad, text_grad)


def solution(mesh):
    placed = (
        P(("grp", "dp"), None),
        P(("grp", "dp")),
        P(("grp", "dp")),
        P(),
        P("dp", None),
        P(None, "dp"),
        P(),
        P(),
        P(),
        P(),
        P(("grp", "dp"), None),
        P(),
        P(),
        P(),
    )
    return jax.shard_map(
        per_device,
        mesh=mesh,
        in_specs=placed,
        out_specs=(P(), P(("grp", "dp"), None), P(("grp", "dp"), None)),
        check_vma=False,
    )
```

profile of v0, /device:TPU:1, one launch (start us, length us, event | category | flops | bytes accessed | tf_op | source)
XLA Modules:
  0.0 1442.0 jit_solution(9616773653495992021)
XLA Ops:
  13.3 3.7 gather_fusion.3
  18.6 7.7 collective-permute-start.1
  27.0 3.7 gather_fusion.4
  32.4 2.9 collective-permute-start.2
  36.0 3.7 gather_fusion.2
  41.4 4.9 collective-permute-start
  48.4 3.7 gather_fusion.1
  52.2 5.2 copy.26
  58.2 2.5 compare_select_fusion.1
  61.6 15.9 %collective-permute-done = bf16[256,1152]{1,0:T(8,128)(2,1)} collective-permute-done((bf16[256,1152]{1,0:T(8,128)(2,1)}, bf16[256,1152]{1,0:T(8,128)(2,1)}, u32[]{:S(2)}, u32[]{:S(2)}) %collective-permute-start) | collective-permute-done | bytes 589856 | tf_op jit(solution)/shard_map/ppermute | solution.py:17
  77.5 3.1 pad_maximum_fusion
  80.6 5.7 gather_fusion
  89.8 633.6 %all-gather.11.cloned.1.call-done = bf16[256,4,1152]{2,1,0:T(4,128)(2,1)} async-done(((bf16[1,4,1152]{2,1,0:T(4,128)(2,1)}), bf16[256,4,1152]{2,1,0:T(4,128)(2,1)}) %all-gather.11.cloned.1.call-update) | async-done | bytes 2359312 | tf_op jit(solution)/shard_map/all_gather | solution.py:128
  723.4 4.9 reshape.247
  728.3 203.7 %all-gather.7.cloned.1.call-done = bf16[32,36,4304]{2,1,0:T(8,128)(2,1)} async-done(((bf16[1,36,4304]{2,1,0:T(8,128)(2,1)}), bf16[32,36,4304]{2,1,0:T(8,128)(2,1)}) %all-gather.7.cloned.1.call-update) | async-done | bytes 9916432 | tf_op jit(solution)/shard_map/all_gather | solution.py:26
  932.0 14.5 %reshape.243 = bf16[1152,4304]{1,0:T(8,128)(2,1)} reshape(bf16[32,36,4304]{2,1,0:T(8,128)(2,1)} %all-gather.7.cloned.1.call-done) | data formatting | bytes 19832832
  946.5 167.4 %all-gather.9.cloned.1.call-done = bf16[32,36,4304]{2,1,0:T(8,128)(2,1)} async-done(((bf16[1,36,4304]{2,1,0:T(8,128)(2,1)}), bf16[32,36,4304]{2,1,0:T(8,128)(2,1)}) %all-gather.9.cloned.1.call-update) | async-done | bytes 9916432 | tf_op jit(solution)/shard_map/all_gather | solution.py:31
  1113.9 14.4 reshape.245
  1128.3 23.9 %fusion.16 = bf16[512,1152]{1,0:T(8,128)(2,1)} fusion(bf16[1152,4304]{1,0:T(8,128)(2,1)} %reshape.245, bf16[1152,4304]{1,0:T(8,128)(2,1)} %reshape.243, f32[1152]{0:T(1024)S(1)} %copy-done.5, f32[512]{0:T(512)S(1)} %add_rsqrt_fusion, f32[512]{0:T(512)S(1)} %broadcast_multiply_fusion, bf16[512,1152]{1,0:T(8,128)(2,1)} %gather_fusion, ...), kind=kOutput, calls=%fused_computation.22 | convolution fusion | flops 10180141056 | bytes 22201344 | tf_op jit(solution)/shard_map/dot_general | solution.py:29
  1152.2 2.7 fusion.30
  1157.1 2.6 fusion.31
  1163.7 3.1 fusion.77
  1166.8 74.5 %psum.7 = f32[]{:T(128)} all-reduce(f32[]{:T(128)} %get-tuple-element.18), channel_id=1, replica_groups=mesh['grp'=8,'dp'=32] {'grp','dp'}, use_global_device_ids=true, to_apply=%region_9.11 | all-reduce | flops 1 | bytes 8 | tf_op jit(solution)/shard_map/psum | solution.py:160
  1245.0 187.0 %all-reduce.3.cloned.1.call-done = f32[1024,1152]{1,0:T(8,128)} async-done(((f32[1024,1152]{1,0:T(8,128)}), f32[1024,1152]{1,0:T(8,128)}) %all-reduce.3.cloned.1.call-update) | async-done | bytes 4718608
  (72 shorter events, 29.8 us)
Async XLA Ops:
  7.2 1145.0 %copy-start = (bf16[1152,1152]{1,0:T(8,128)(2,1)S(1)}, bf16[1152,1152]{1,0:T(8,128)(2,1)}, u32[]{:S(2)}) copy-start(bf16[1152,1152]{1,0:T(8,128)(2,1)} %param.23) | copy-start | bytes 7962628
  7.2 716.2 %all-gather.11.cloned.1.call-start = ((), (), s32[]{:S(2)}) async-start(), calls=%async_computation.2 | async-start | bytes 2368512 | tf_op jit(solution)/shard_map/all_gather | solution.py:128
  9.6 922.4 %all-gather.7.cloned.1.call-start = ((), (), s32[]{:S(2)}) async-start(), calls=%async_computation | async-start | bytes 11489280 | tf_op jit(solution)/shard_map/all_gather | solution.py:26
  10.4 1103.5 %all-gather.9.cloned.1.call-start = ((), (), s32[]{:S(2)}) async-start(), calls=%async_computation.1 | async-start | bytes 11489280 | tf_op jit(solution)/shard_map/all_gather | solution.py:31
  11.1 1420.8 %all-reduce.3.cloned.1.call-start = ((), (), s32[]{:S(2)}) async-start(), calls=%async_computation.3 | async-start | bytes 9437184
  18.6 43.0 %collective-permute-start.1 = (bf16[256,1152]{1,0:T(8,128)(2,1)}, bf16[256,1152]{1,0:T(8,128)(2,1)}, u32[]{:S(2)}, u32[]{:S(2)}) collective-permute-start(bf16[256,1152]{1,0:T(8,128)(2,1)} %broadcast_select_fusion.2), channel_id=1, source_target_pairs={{0,16},{1,17},{2,18},{3,19},{4,20},{5,21},{6,22},{7,23},{8,24},{9,... | collective-permute-start | bytes 1769480 | tf_op jit(solution)/shard_map/ppermute | solution.py:17
  32.4 29.2 %collective-permute-start.2 = (bf16[256,1152]{1,0:T(8,128)(2,1)}, bf16[256,1152]{1,0:T(8,128)(2,1)}, u32[]{:S(2)}, u32[]{:S(2)}) collective-permute-start(bf16[256,1152]{1,0:T(8,128)(2,1)} %broadcast_select_fusion.1), channel_id=1, source_target_pairs={{0,8},{1,9},{2,10},{3,11},{4,12},{5,13},{6,14},{7,15},{8,16},{9,17... | collective-permute-start | bytes 1769480 | tf_op jit(solution)/shard_map/ppermute | solution.py:17
  36.0 11.6 copy-start.6
  41.4 36.1 %collective-permute-start = (bf16[256,1152]{1,0:T(8,128)(2,1)}, bf16[256,1152]{1,0:T(8,128)(2,1)}, u32[]{:S(2)}, u32[]{:S(2)}) collective-permute-start(bf16[256,1152]{1,0:T(8,128)(2,1)} %broadcast_select_fusion.3), channel_id=1, source_target_pairs={{0,24},{1,25},{2,26},{3,27},{4,28},{5,29},{6,30},{7,31},{8,0},{9,1... | collective-permute-start | bytes 1769480 | tf_op jit(solution)/shard_map/ppermute | solution.py:17
  52.1 5.3 copy-start.3
  946.5 181.8 %copy-start.5 = (f32[1152]{0:T(1024)S(1)}, f32[1152]{0:T(1024)}, u32[]{:S(2)}) copy-start(f32[1152]{0:T(1024)} %param.19) | copy-start | bytes 13828
  1128.3 23.9 %copy-start.4 = (bf16[1152]{0:T(1024)(128)(2,1)S(1)}, bf16[1152]{0:T(1024)(128)(2,1)}, u32[]{:S(2)}) copy-start(bf16[1152]{0:T(1024)(128)(2,1)} %param.22) | copy-start | bytes 6916
  1159.9 2.5 copy-start.1
  1166.8 265.1 %copy-start.2 = (bf16[4,1152]{1,0:T(4,128)(2,1)S(1)}, bf16[4,1152]{1,0:T(4,128)(2,1)}, u32[]{:S(2)}) copy-start(bf16[4,1152]{1,0:T(4,128)(2,1)} %param.26) | copy-start | bytes 27652
Sparse Core Ops, SparseCore 0:
  10.5 712.8 all-gather.10
  726.7 205.1 all-gather.6
  935.4 178.4 all-gather.8
  1166.9 264.9 all-reduce.2
where the time goes:
time: 1440 us
  waiting for transfers between devices  1210 us (84%)
  blocking collectives  74.5 us (5%)
  local copies, waits for them, and re-layouts  62.1 us (4%)
  matrix products  40 us (3%)
  other arithmetic  23.7 us (2%)
  between operations  17.1 us (1%)
  starting transfers between devices  15.7 us (1%)
    all_gather x1, waiting for transfers between devices, per_device(): text_all = lax.all_gather(text_low, ('grp', 'dp'), axis=0, tiled=True)  634 us
    all_gather x1, waiting for transfers between devices, feed_forward(): lax.all_gather(mlp_in, 'dp', axis=0, tiled=True)  204 us
    unnamed x5, waiting for transfers between devices  188 us
    all_gather x1, waiting for transfers between devices, feed_forward(): lax.all_gather(mlp_out, 'dp', axis=1, tiled=True)  167 us
    psum x1, blocking collectives, per_device(): loss_value = lax.psum(partial_loss, ('grp', 'dp')) / text_all.shape[0]  74.5 us
    unnamed x18, local copies, waits for them, and re-layouts  39.2 us
  transfers between devices with their start and end apart: 7, of which 5 were waited for; matrix products, arithmetic and copies ran while one was open for 5% of the time, Pallas kernels for 0%

commit v1 on v0

v1 whole, which is shorter than its diff:
```python
import math

import jax
import jax.numpy as jnp
from jax import lax
from jax.experimental import pallas as pl
from jax.experimental.pallas import tpu as pltpu
from jax.sharding import PartitionSpec as P

MESH = pl.DeviceIdType.MESH
F32 = jnp.float32
BF16 = jnp.bfloat16
I32 = jnp.int32

EPSILON = 1e-06
D = 1152
FF = 4304
HEAD_DIM = 72
HEADS = 16
PACK = 1024
TEXTS = 1024
SHARD = 36
SLOT_ROWS = 48
LANES = 128
CHUNKS = 17
HALF = CHUNKS * LANES
BLOCK = 4 * SHARD
GROUP = 4 * BLOCK
TILE = 256

LAG_A, LAG_B, LAG_C, LAG_D, LAG_E = 1, 2, 3, 4, 5
TICKS = CHUNKS + LAG_E

Z, A_MINUS, A_PLUS, A_FAR, B_MINUS, B_PLUS, B_FAR, SIB = range(8)

NT = (((1,), (1,)), ((), ()))


def gelu(hidden):
    c1 = math.sqrt(2.0 / math.pi)
    c2 = c1 * 0.044715
    inner = hidden * (c1 + c2 * (hidden * hidden))
    half = 0.5 * hidden
    return (half + half * jnp.tanh(inner)).astype(BF16)


def kernel(
    patches, counts, offsets, gain, win, woutt, probe, key_w, value_w, out_w, text, labels, scale, bias,
    loss_out, igrad_out, tgrad_out,
    xbuf, normed, acc, G, a2a_s, a2a_r, compact, T, line_f, tx_s, tx_r, ix_s, ix_r, PI, tcol,
    ps_s, ps_r, ig_s, ig_r, cn_s, cn_r, hk, kw, vw, ow, ilab, tlab, ls_s, ls_r,
    loc_sem, g_ss, g_rs, x_ss, x_rs, tx_ss, tx_rs, ty_ss, ty_rs, tz_ss, tz_rs, ts_ss, ts_rs,
    ix_ss, ix_rs, iy_ss, iy_rs, ps_ss, ps_rs, ig_ss, ig_rs, cn_ss, cn_rs,
    l1_ss, l1_rs, l2_ss, l2_rs, l3_ss, l3_rs,
):
    g = lax.axis_index("grp")
    d = lax.axis_index("dp")
    k = lax.rem(g, 2)
    zl = lax.div(g, 2)
    x = lax.rem(d, 4)
    y = lax.rem(lax.div(d, 4), 4)
    zh = lax.div(d, 16)
    z = zh * 4 + zl

    def dev(x_, y_, z_, k_):
        return (lax.rem(z_, 4) * 2 + k_, lax.div(z_, 4) * 16 + y_ * 4 + x_)

    def m4(v):
        return lax.rem(v, 4)

    def m8(v):
        return lax.rem(v, 8)

    sib = dev(x, y, z, 1 - k)
    xs = [dev(m4(x + i), y, z, k) for i in (1, 2, 3)]
    zs = [dev(x, y, m8(z + i), k) for i in range(1, 8)]
    group_dev = [(g, lax.rem(d + 8 * j, 32)) for j in range(4)]

    def rcopy(src, dst, ss, rs, to):
        return pltpu.make_async_remote_copy(
            src_ref=src, dst_ref=dst, send_sem=ss, recv_sem=rs, device_id=to, device_id_type=MESH
        )

    def wait_recv(ref, rs):
        rcopy(ref, ref, loc_sem.at[0], rs, sib).wait_recv()

    def wait_send(ref, ss):
        rcopy(ref, ref, ss, loc_sem.at[0], sib).wait_send()

    barrier = pltpu.get_barrier_semaphore()
    partners = list(xs) + list(zs) + [sib]
    for i in (1, 2, 3):
        for c_ in (0, 1):
            partners.append(dev(x, m4(y + i), z, c_))
    partners.append(dev(x, m4(y + 2), m8(z + 4), k))
    for p in partners:
        pl.semaphore_signal(barrier, inc=1, device_id=p, device_id_type=MESH)

    local = [
        pltpu.make_async_copy(patches, xbuf, loc_sem.at[1]),
        pltpu.make_async_copy(key_w, kw, loc_sem.at[2]),
        pltpu.make_async_copy(value_w, vw, loc_sem.at[3]),
        pltpu.make_async_copy(out_w, ow, loc_sem.at[4]),
    ]
    for cp in local:
        cp.start()

    source = k == zh

    @pl.when(source)
    def _():
        for part in range(4):
            shard = win if part < 2 else woutt
            if part % 2 == 0:
                a2a_s[part, 0:SHARD, :] = shard[:, 0:HALF]
            else:
                a2a_s[part, :, HALF - LANES:HALF] = jnp.zeros((SLOT_ROWS, LANES), BF16)
                a2a_s[part, 0:SHARD, 0:FF - HALF] = shard[:, HALF:FF]

    text_wide = text[...].astype(F32)
    text_inv = lax.rsqrt(jnp.sum(text_wide * text_wide, axis=1, keepdims=True) + EPSILON)
    text_unit = text_wide * text_inv
    tx_s[...] = jnp.zeros((16, D), BF16)
    tx_s[0:4, :] = text_unit.astype(BF16)
    for j in range(4):
        cn_s[j] = jnp.full((8, LANES), counts[j], I32)

    pl.semaphore_wait(barrier, len(partners))

    @pl.when(source)
    def _():
        for i in range(3):
            to_x = m4(x + i + 1)
            rcopy(a2a_s.at[to_x], a2a_r.at[x], x_ss.at[i], x_rs.at[x], xs[i]).start()
        a2a_r[x] = a2a_s[x]

    for i in range(3):
        rcopy(tx_s, tx_r.at[x], tx_ss.at[i], tx_rs.at[x], xs[i]).start()
    tx_r[x] = tx_s[...]
    for j in (1, 2, 3):
        rcopy(cn_s.at[j], cn_r.at[j], cn_ss.at[j], cn_rs.at[j], group_dev[j]).start()
    cn_r[0] = cn_s[0]

    a = jnp.where(k == 0, y, x)
    b = jnp.where(k == 0, x, y)

    def along(axis_is_a, step):
        move_y = jnp.where(k == 0, 1, 0) if axis_is_a else jnp.where(k == 0, 0, 1)
        return dev(m4(x + (1 - move_y) * step), m4(y + move_y * step), z, k)

    a_plus, a_minus = along(True, 1), along(True, 3)
    b_plus, b_minus = along(False, 1), along(False, 3)

    def a_block(c, at):
        return G.at[c, k, b, pl.ds(pl.multiple_of(at * BLOCK, 16), BLOCK), :]

    def b_group(c, at):
        return G.at[c, k, at]

    @pl.when(source)
    def _():
        for i in (1, 2, 3):
            s = m4(x + i)
            wait_recv(a2a_r.at[s], x_rs.at[s])
        for s in range(4):
            compact[s * SHARD:(s + 1) * SHARD, :] = a2a_r[s, 0:SHARD, :].astype(F32)
        for c in range(CHUNKS):
            G[c, k, b, pl.ds(pl.multiple_of(a * BLOCK, 16), BLOCK), :] = compact[
                :, c * LANES:(c + 1) * LANES
            ].astype(BF16)

    edge = jnp.logical_or(zl == 0, zl == 3)
    outward = jnp.where(zl == 3, 1, 7)
    z_to = dev(x, y, m8(z + jnp.where(source, outward, 8 - outward)), k)

    def t_block(zl_, k_, zh_):
        return T.at[zl_, k_, zh_]

    def z_parts(step):
        zz = m8(z + step)
        return m4(zz), lax.div(zz, 4)

    def text_ring(step):
        zl_, zh_ = z_parts(step)
        return T.at[zl_, k, zh_]

    z_plus, z_minus = zs[0], zs[6]
    own_t = pl.ds(pl.multiple_of(y * 16, 16), 16)

    def gather_line(received, wide):
        for s in range(4):
            wide[4 * s:4 * s + 4, :] = received[s, 0:4, :].astype(F32)
        return wide[...].astype(BF16)

    def label_cols(ids):
        rows = ids.shape[0]
        lanes = lax.broadcasted_iota(I32, (rows, TEXTS), 1)
        row = jnp.broadcast_to(labels[...].astype(F32), (rows, TEXTS))
        return jnp.sum(jnp.where(lanes == ids, row, 0.0), axis=1, keepdims=True)

    def tick(t, carry):
        @pl.when(t < CHUNKS)
        def _():
            c = t
            own = a_block(c, a)

            @pl.when(jnp.logical_not(source))
            def _():
                wait_recv(own, g_rs.at[Z, c])

            @pl.when(edge)
            def _():
                rcopy(own, own, g_ss.at[Z, c], g_rs.at[Z, c], z_to).start()

            rcopy(own, own, g_ss.at[A_MINUS, c], g_rs.at[A_MINUS, c], a_plus).start()
            rcopy(own, own, g_ss.at[A_PLUS, c], g_rs.at[A_PLUS, c], a_minus).start()

        @pl.when(jnp.logical_and(t >= LAG_A, t < CHUNKS + LAG_A))
        def _():
            c = t - LAG_A
            even = lax.rem(c, 2) == 0
            blk = a_block(c, m4(a + jnp.where(even, 3, 1)))
            wait_recv(blk, g_rs.at[jnp.where(even, A_MINUS, A_PLUS), c])
            to = tuple(jnp.where(even, p, m) for p, m in zip(a_plus, a_minus))
            rcopy(blk, blk, g_ss.at[A_FAR, c], g_rs.at[A_FAR, c], to).start()

        @pl.when(jnp.logical_and(t >= LAG_B, t < CHUNKS + LAG_B))
        def _():
            c = t - LAG_B
            even = lax.rem(c, 2) == 0
            wait_recv(a_block(c, m4(a + jnp.where(even, 1, 3))), g_rs.at[jnp.where(even, A_PLUS, A_MINUS), c])
            wait_recv(a_block(c, m4(a + 2)), g_rs.at[A_FAR, c])
            grp = b_group(c, b)
            rcopy(grp, grp, g_ss.at[B_MINUS, c], g_rs.at[B_MINUS, c], b_plus).start()
            rcopy(grp, grp, g_ss.at[B_PLUS, c], g_rs.at[B_PLUS, c], b_minus).start()

        @pl.when(jnp.logical_and(t >= LAG_C, t < CHUNKS + LAG_C))
        def _():
            c = t - LAG_C
            even = lax.rem(c, 2) == 0
            grp = b_group(c, m4(b + jnp.where(even, 3, 1)))
            wait_recv(grp, g_rs.at[jnp.where(even, B_MINUS, B_PLUS), c])
            to = tuple(jnp.where(even, p, m) for p, m in zip(b_plus, b_minus))
            rcopy(grp, grp, g_ss.at[B_FAR, c], g_rs.at[B_FAR, c], to).start()

        @pl.when(jnp.logical_and(t >= LAG_D, t < CHUNKS + LAG_D))
        def _():
            c = t - LAG_D
            even = lax.rem(c, 2) == 0
            wait_recv(b_group(c, m4(b + jnp.where(even, 1, 3))), g_rs.at[jnp.where(even, B_PLUS, B_MINUS), c])
            wait_recv(b_group(c, m4(b + 2)), g_rs.at[B_FAR, c])
            half = G.at[c, k]
            rcopy(half, half, g_ss.at[SIB, c], g_rs.at[SIB, c], sib).start()

        @pl.when(t == 0)
        def _():
            for i in (1, 2, 3):
                s = m4(x + i)
                wait_recv(tx_r.at[s], tx_rs.at[s])
            T[zl, k, zh, own_t, :] = gather_line(tx_r, line_f)
            blk = T.at[zl, k, zh, own_t, :]
            for i in (1, 2, 3):
                rcopy(blk, blk, ty_ss.at[i - 1], ty_rs.at[y], dev(x, m4(y + i), z, k)).start()

        @pl.when(t == 1)
        def _():
            for i in (1, 2, 3):
                yy = m4(y + i)
                wait_recv(T.at[zl, k, zh, pl.ds(pl.multiple_of(yy * 16, 16), 16), :], ty_rs.at[yy])
            blk = text_ring(0)
            rcopy(blk, blk, tz_ss.at[0, 0], tz_rs.at[0, 0], z_plus).start()
            rcopy(blk, blk, tz_ss.at[1, 0], tz_rs.at[1, 0], z_minus).start()

        for hop in (1, 2):

            @pl.when(t == 1 + 2 * hop)
            def _():
                low, high = text_ring(8 - hop), text_ring(hop)
                wait_recv(low, tz_rs.at[0, hop - 1])
                wait_recv(high, tz_rs.at[1, hop - 1])
                rcopy(low, low, tz_ss.at[0, hop], tz_rs.at[0, hop], z_plus).start()
                rcopy(high, high, tz_ss.at[1, hop], tz_rs.at[1, hop], z_minus).start()

        @pl.when(t == 7)
        def _():
            low, high = text_ring(5), text_ring(3)
            wait_recv(low, tz_rs.at[0, 2])
            wait_recv(high, tz_rs.at[1, 2])

            @pl.when(k == 0)
            def _():
                rcopy(low, low, tz_ss.at[0, 3], tz_rs.at[0, 3], z_plus).start()

            @pl.when(k == 1)
            def _():
                rcopy(high, high, tz_ss.at[0, 3], tz_rs.at[0, 3], z_minus).start()

        @pl.when(t == 9)
        def _():
            wait_recv(text_ring(4), tz_rs.at[0, 3])
            mine = T.at[:, k]
            rcopy(mine, mine, ts_ss.at[0], ts_rs.at[0], sib).start()

        @pl.when(t == 0)
        def _():
            local[0].wait()

        @pl.when(t < PACK // TILE)
        def _():
            sl = pl.ds(pl.multiple_of(t * TILE, TILE), TILE)
            wide = xbuf[sl, :].astype(F32)
            center = jnp.mean(wide, axis=1, keepdims=True)
            off = wide - center
            spread = jnp.mean(off * off, axis=1, keepdims=True)
            normed[sl, :] = (off * lax.rsqrt(spread + EPSILON) * gain[...]).astype(BF16)
            acc[sl, :] = wide

        @pl.when(t == 4)
        def _():
            local[1].wait()
            head_of = lax.div(lax.broadcasted_iota(I32, (HEADS, D), 1), HEAD_DIM)
            own_head = head_of == lax.broadcasted_iota(I32, (HEADS, D), 0)
            block = jnp.where(own_head, jnp.broadcast_to(probe[...].astype(F32), (HEADS, D)), 0.0)
            keys = lax.dot_general(block.astype(BF16), kw[...], NT, preferred_element_type=F32)
            hk[...] = (keys / math.sqrt(HEAD_DIM)).astype(BF16)

            pos = lax.broadcasted_iota(I32, (LANES, 1), 0)
            slot = lax.rem(pos, 4)
            px = lax.rem(lax.div(pos, 4), 4)
            py = lax.rem(lax.div(pos, 16), 4)
            pk = lax.div(pos, 64)
            owner = lax.rem(16 * zh + 4 * py + px + 32 - 8 * slot, 32)
            ids = 4 * ((2 * zl + pk) * 32 + owner) + slot
            hot = lax.broadcasted_iota(I32, (LANES, TEXTS), 1) == ids
            hot = jnp.where(hot, 1.0, 0.0).astype(BF16)
            lab = labels[...]
            high = lax.div(lab, 16)
            low = lab - 16 * high
            pair = jnp.where(
                lax.broadcasted_iota(I32, (16, TEXTS), 0) == 0,
                jnp.broadcast_to(high, (16, TEXTS)),
                jnp.broadcast_to(low, (16, TEXTS)),
            ).astype(F32).astype(BF16)
            rows = lax.dot_general(pair, hot, NT, preferred_element_type=F32)
            ilab[...] = jnp.broadcast_to(16.0 * rows[0:1, :] + rows[1:2, :], (8, LANES))
            tpos = lax.broadcasted_iota(I32, (64, 1), 0)
            tz = lax.div(tpos, 8)
            tid = m4(tz) * 256 + k * 128 + lax.div(tz, 4) * 64 + y * 16 + x * 4 + m4(tpos)
            tlab[...] = jnp.broadcast_to(label_cols(tid), (64, LANES))

        @pl.when(t >= LAG_E)
        def _():
            c = t - LAG_E
            wait_recv(G.at[c, 1 - k], g_rs.at[SIB, c])

            def part(p):
                pieces = [G[c, 0, p]]
                for yy in range(4):
                    pieces.append(G[c, 1, yy, p * BLOCK:(p + 1) * BLOCK, :])
                return jnp.concatenate(pieces, axis=0)

            w1 = jnp.concatenate([part(0), part(1)], axis=1)
            w2 = jnp.concatenate([part(2), part(3)], axis=1)
            for r in range(PACK // TILE):
                sl = slice(r * TILE, (r + 1) * TILE)
                hidden = jnp.dot(normed[sl, :], w1, preferred_element_type=F32)
                acc[sl, :] += lax.dot_general(gelu(hidden), w2, NT, preferred_element_type=F32)

        return carry

    lax.fori_loop(0, TICKS, tick, 0)

    states = normed
    states[...] = acc[...].astype(BF16)
    scores = lax.dot_general(hk[...], states[...], NT, preferred_element_type=F32)
    row = lax.broadcasted_iota(I32, (HEADS, PACK), 1)
    all_weights = []
    for j in range(4):
        if j > 0:
            wait_recv(cn_r.at[j], cn_rs.at[j])
        first = offsets[j]
        count = cn_r[j][0:1, 0:1]
        member = jnp.logical_and(row >= first, row < first + count)
        masked = jnp.where(member, scores, -1e30)
        highest = jnp.max(masked, axis=1, keepdims=True)
        raised = jnp.exp(masked - highest)
        all_weights.append(raised / jnp.sum(raised, axis=1, keepdims=True))
    weights = jnp.concatenate(all_weights, axis=0).astype(BF16)
    mean_states = jnp.dot(weights, states[...], preferred_element_type=F32).astype(BF16)
    local[2].wait()
    local[3].wait()
    full = jnp.dot(mean_states, vw[...], preferred_element_type=F32)
    head_of = lax.div(lax.broadcasted_iota(I32, (HEADS, D), 1), HEAD_DIM)
    own_head = head_of == lax.broadcasted_iota(I32, (HEADS, D), 0)
    values = [
        jnp.sum(jnp.where(own_head, full[HEADS * j:HEADS * (j + 1), :], 0.0), axis=0, keepdims=True)
        for j in range(4)
    ]
    mixed = jnp.concatenate(values + [jnp.zeros((12, D), F32)], axis=0).astype(BF16)
    pooled = jnp.dot(mixed, ow[...], preferred_element_type=F32)[0:8, :]
    image_inv = lax.rsqrt(jnp.sum(pooled * pooled, axis=1, keepdims=True) + EPSILON)
    image_unit = pooled * image_inv
    ix_s[...] = jnp.concatenate([image_unit, jnp.zeros((8, D), F32)], axis=0).astype(BF16)

    for i in range(3):
        rcopy(ix_s, ix_r.at[x], ix_ss.at[i], ix_rs.at[x], xs[i]).start()
    ix_r[x] = ix_s[...]

    mult = scale[0]
    shift = bias[0]

    wait_recv(T.at[:, 1 - k], ts_rs.at[0])
    texts = T[...].reshape(TEXTS, D)
    own_logits = mult * lax.dot_general(ix_s[...], texts, NT, preferred_element_type=F32) + shift
    slot = lax.broadcasted_iota(I32, (16, 1), 0)
    slot4 = m4(slot)
    own_ids = 4 * (g * 32 + lax.rem(d + 32 - 8 * slot4, 32)) + slot4
    own_lab = label_cols(own_ids)
    sign = jnp.where(own_lab == labels[...].astype(F32), 1.0, -1.0)
    signed = sign * own_logits
    terms = jnp.log1p(jnp.exp(-jnp.abs(signed))) + jnp.maximum(-signed, 0.0)
    terms = jnp.where(slot < 4, terms, 0.0)
    part_loss = jnp.sum(jnp.sum(terms, axis=1, keepdims=True), axis=0, keepdims=True)
    ls_s[0] = jnp.broadcast_to(part_loss, (8, LANES))
    for i in range(3):
        rcopy(ls_s.at[0], ls_r.at[0, x], l1_ss.at[i], l1_rs.at[x], xs[i]).start()
    ls_r[0, x] = ls_s[0]

    for i in (1, 2, 3):
        s = m4(x + i)
        wait_recv(ix_r.at[s], ix_rs.at[s])
    PI[k, own_t, :] = gather_line(ix_r, line_f)
    others = [(m4(y + i), c_) for i in (1, 2, 3) for c_ in (0, 1)]
    to_plane = [dev(x, yy, z, c_) for yy, c_ in others] + [sib]
    blk = PI.at[k, own_t, :]
    for i, to in enumerate(to_plane):
        rcopy(blk, blk, iy_ss.at[i], iy_rs.at[k, y], to).start()

    for i in (1, 2, 3):
        s = m4(x + i)
        wait_recv(ls_r.at[0, s], l1_rs.at[s])
    ls_s[1] = ls_r[0, 0] + ls_r[0, 1] + ls_r[0, 2] + ls_r[0, 3]
    me8 = k * 4 + y
    for i, to in enumerate(to_plane):
        rcopy(ls_s.at[1], ls_r.at[1, me8], l2_ss.at[i], l2_rs.at[me8], to).start()
    ls_r[1, me8] = ls_s[1]

    own_slope = (mult * -sign * jax.nn.sigmoid(-signed)).astype(BF16)
    image_push = jnp.dot(own_slope, texts, preferred_element_type=F32)[0:8, :]
    image_grad = (
        image_push - image_unit * jnp.sum(image_unit * image_push, axis=1, keepdims=True)
    ) * image_inv
    for j in range(4):
        ig_s[j] = image_grad[j:j + 1, :]
    for j in (1, 2, 3):
        rcopy(ig_s.at[j], ig_r.at[j], ig_ss.at[j], ig_rs.at[j], group_dev[4 - j]).start()
    ig_r[0] = ig_s[0]

    for zz in range(8):
        block = T[zz % 4, k, zz // 4, own_t, :].astype(F32)
        mine = jnp.zeros((4, D), F32)
        for s in range(4):
            mine = mine + jnp.where(x == s, 1.0, 0.0) * block[4 * s:4 * s + 4, :]
        tcol[8 * zz:8 * zz + 4, :] = mine
        tcol[8 * zz + 4:8 * zz + 8, :] = jnp.zeros((4, D), F32)

    for yy, c_ in others + [(y, 1 - k)]:
        wait_recv(PI.at[c_, pl.ds(pl.multiple_of(yy * 16, 16), 16), :], iy_rs.at[c_, yy])
    plane = PI[...].reshape(LANES, D)
    plane_logits = mult * lax.dot_general(
        tcol[...].astype(BF16), plane, NT, preferred_element_type=F32
    ) + shift
    plane_sign = jnp.where(tlab[...] == ilab[0:1, :], 1.0, -1.0)
    plane_slope = (mult * -plane_sign * jax.nn.sigmoid(-plane_sign * plane_logits)).astype(BF16)
    push = jnp.dot(plane_slope, plane, preferred_element_type=F32)
    for zz in range(8):
        ps_s[zz] = push[8 * zz:8 * zz + 8, :]
    for i in range(7):
        to_z = m8(z + i + 1)
        rcopy(ps_s.at[to_z], ps_r.at[z], ps_ss.at[i], ps_rs.at[z], zs[i]).start()
    ps_r[z] = ps_s[z]

    for yy, c_ in others + [(y, 1 - k)]:
        wait_recv(ls_r.at[1, c_ * 4 + yy], l2_rs.at[c_ * 4 + yy])
    total = ls_r[1, 0]
    for i in range(1, 8):
        total = total + ls_r[1, i]
    ls_s[2] = total
    for i in range(7):
        rcopy(ls_s.at[2], ls_r.at[2, z], l3_ss.at[i], l3_rs.at[z], zs[i]).start()
    ls_r[2, z] = ls_s[2]

    for j in (1, 2, 3):
        wait_recv(ig_r.at[j], ig_rs.at[j])
    for j in range(4):
        igrad_out[j:j + 1, :] = ig_r[j]

    for i in range(1, 8):
        zz = m8(z + i)
        wait_recv(ps_r.at[zz], ps_rs.at[zz])
    text_push = ps_r[0]
    for i in range(1, 8):
        text_push = text_push + ps_r[i]
    text_push = text_push[0:4, :]
    tgrad_out[...] = (
        text_push - text_unit * jnp.sum(text_unit * text_push, axis=1, keepdims=True)
    ) * text_inv

    for i in range(1, 8):
        zz = m8(z + i)
        wait_recv(ls_r.at[2, zz], l3_rs.at[zz])
    total = ls_r[2, 0]
    for i in range(1, 8):
        total = total + ls_r[2, i]
    loss_out[...] = total[0:1, 0:1] / float(TEXTS)

    def drain(c, carry):
        own = a_block(c, a)

        @pl.when(edge)
        def _():
            wait_send(own, g_ss.at[Z, c])

        for kind in (A_MINUS, A_PLUS, A_FAR):
            wait_send(own, g_ss.at[kind, c])
        for kind in (B_MINUS, B_PLUS, B_FAR):
            wait_send(b_group(c, b), g_ss.at[kind, c])
        wait_send(G.at[c, k], g_ss.at[SIB, c])
        return carry

    lax.fori_loop(0, CHUNKS, drain, 0)

    @pl.when(source)
    def _():
        for i in range(3):
            wait_send(a2a_s.at[0], x_ss.at[i])

    for i in range(3):
        wait_send(tx_s, tx_ss.at[i])
        wait_send(T.at[zl, k, zh, own_t, :], ty_ss.at[i])
        wait_send(ix_s, ix_ss.at[i])
        wait_send(ls_s.at[0], l1_ss.at[i])
        wait_send(cn_s.at[i + 1], cn_ss.at[i + 1])
        wait_send(ig_s.at[i + 1], ig_ss.at[i + 1])
        wait_send(text_ring(0), tz_ss.at[0, i])
        wait_send(text_ring(0), tz_ss.at[1, i])
    wait_send(text_ring(0), tz_ss.at[0, 3])
    wait_send(T.at[:, k], ts_ss.at[0])
    for i in range(7):
        wait_send(PI.at[k, own_t, :], iy_ss.at[i])
        wait_send(ls_s.at[1], l2_ss.at[i])
        wait_send(ps_s.at[0], ps_ss.at[i])
        wait_send(ls_s.at[2], l3_ss.at[i])


def per_device(
    patches, patch_counts, pack_offsets, norm_gain, mlp_in, mlp_out, probe_query, key_weight,
    value_weight, out_weight, text_embed, pair_label, logit_scale, logit_bias,
):
    vmem = pl.BlockSpec(memory_space=pltpu.VMEM)
    smem = pl.BlockSpec(memory_space=pltpu.SMEM)
    anywhere = pl.BlockSpec(memory_space=pl.ANY)
    dma = pltpu.SemaphoreType.DMA
    loss, image_grad, text_grad = pl.pallas_call(
        kernel,
        out_shape=(
            jax.ShapeDtypeStruct((1, 1), F32),
            jax.ShapeDtypeStruct((4, D), F32),
            jax.ShapeDtypeStruct((4, D), F32),
        ),
        in_specs=[
            anywhere, smem, smem, vmem, vmem, vmem, vmem, anywhere, anywhere, anywhere, vmem, vmem, smem, smem,
        ],
        out_specs=(vmem, vmem, vmem),
        scratch_shapes=[
            pltpu.VMEM((PACK, D), BF16),
            pltpu.VMEM((PACK, D), BF16),
            pltpu.VMEM((PACK, D), F32),
            pltpu.VMEM((CHUNKS, 2, 4, GROUP, LANES), BF16),
            pltpu.VMEM((4, SLOT_ROWS, HALF), BF16),
            pltpu.VMEM((4, SLOT_ROWS, HALF), BF16),
            pltpu.VMEM((BLOCK, HALF), F32),
            pltpu.VMEM((4, 2, 2, 64, D), BF16),
            pltpu.VMEM((16, D), F32),
            pltpu.VMEM((16, D), BF16),
            pltpu.VMEM((4, 16, D), BF16),
            pltpu.VMEM((16, D), BF16),
            pltpu.VMEM((4, 16, D), BF16),
            pltpu.VMEM((2, 64, D), BF16),
            pltpu.VMEM((64, D), F32),
            pltpu.VMEM((8, 8, D), F32),
            pltpu.VMEM((8, 8, D), F32),
            pltpu.VMEM((4, 1, D), F32),
            pltpu.VMEM((4, 1, D), F32),
            pltpu.VMEM((4, 8, LANES), I32),
            pltpu.VMEM((4, 8, LANES), I32),
            pltpu.VMEM((HEADS, D), BF16),
            pltpu.VMEM((D, D), BF16),
            pltpu.VMEM((D, D), BF16),
            pltpu.VMEM((D, D), BF16),
            pltpu.VMEM((8, LANES), F32),
            pltpu.VMEM((64, LANES), F32),
            pltpu.VMEM((3, 8, LANES), F32),
            pltpu.VMEM((3, 8, 8, LANES), F32),
            dma((5,)),
            dma((8, CHUNKS)), dma((8, CHUNKS)),
            dma((3,)), dma((4,)),
            dma((3,)), dma((4,)),
            dma((3,)), dma((4,)),
            dma((2, 4)), dma((2, 4)),
            dma((1,)), dma((1,)),
            dma((3,)), dma((4,)),
            dma((7,)), dma((2, 4)),
            dma((7,)), dma((8,)),
            dma((4,)), dma((4,)),
            dma((4,)), dma((4,)),
            dma((3,)), dma((4,)),
            dma((7,)), dma((8,)),
            dma((7,)), dma((8,)),
        ],
        compiler_params=pltpu.CompilerParams(
            collective_id=0, has_side_effects=True, vmem_limit_bytes=62 * 2**20
        ),
        cost_estimate=pl.CostEstimate(
            flops=4 * PACK * D * FF, bytes_accessed=12 * 2**20, transcendentals=PACK * FF
        ),
        name="pooled_loss",
    )(
        patches, patch_counts, pack_offsets, norm_gain.reshape(1, D), mlp_in, mlp_out.T,
        probe_query.reshape(1, D), key_weight, value_weight, out_weight, text_embed,
        pair_label.reshape(1, TEXTS), logit_scale, logit_bias,
    )
    return loss.reshape(()), image_grad, text_grad


def solution(mesh):
    placed = (
        P(("grp", "dp"), None), P(("grp", "dp")), P(("grp", "dp")), P(), P("dp", None), P(None, "dp"),
        P(), P(), P(), P(), P(("grp", "dp"), None), P(), P(), P(),
    )
    return jax.shard_map(
        per_device,
        mesh=mesh,
        in_specs=placed,
        out_specs=(P(), P(("grp", "dp"), None), P(("grp", "dp"), None)),
        check_vma=False,
    )
```

time: 1440 us -> 153 us (0.11)
  waiting for transfers between devices: 1210 us -> 0 us
  Pallas kernels: 0 us -> 144 us
  blocking collectives: 74.5 us -> 0 us
  local copies, waits for them, and re-layouts: 62.1 us -> 5.23 us
  matrix products: 40 us -> 0 us
  other arithmetic: 23.7 us -> 0 us
  starting transfers between devices: 15.7 us -> 0 us
    all_gather x3 -> x0, waiting for transfers between devices: 1000 us -> none  [the longest x1 634 us: per_device(): text_all = lax.all_gather(text_low, ('grp', 'dp'), axis=0, tiled=True)]
    unnamed x5 -> x0, waiting for transfers between devices: 188 us -> none
    pallas_call x0 -> x1, Pallas kernels: none -> 144 us  [per_device(): pl.pallas_call(kernel, out_shape=(jax.ShapeDtypeStruct((1, 1), F32), jax....]
    psum x1 -> x0, blocking collectives: 74.5 us -> none  [per_device(): loss_value = lax.psum(partial_loss, ('grp', 'dp')) / text_all.shape[0]]
    dot_general x8 -> x0, matrix products: 40 us -> none  [the longest x1 23.9 us: feed_forward(): jnp.dot(active, lax.all_gather(mlp_out, 'dp', axis=1, tiled=True), prefer...]
    unnamed x18 -> x2, local copies, waits for them, and re-layouts: 39.2 us -> 2.66 us
    gather x6 -> x0, local copies, waits for them, and re-layouts: 21.1 us -> none  [the longest x4 14.8 us: per_device(): window = jnp.take(patches, picked, axis=0)]
    ppermute x3 -> x0, waiting for transfers between devices: 15.9 us -> none  [from_behind(): lax.ppermute(value, axis, [(i, (i + by) % devices) for i in range(devices)])]
  transfers between devices with their start and end apart: 7 -> 0, of which waited for: 5 -> 0; matrix products, arithmetic and copies ran while one was open for 5% -> 0% of each run, Pallas kernels for 0% -> 0%
where the time goes in v1:
time: 153 us
  Pallas kernels  144 us (94%)
  local copies, waits for them, and re-layouts  5.23 us (3%)
  between operations  3.68 us (2%)
    pallas_call x1, Pallas kernels, per_device(): pl.pallas_call(kernel, out_shape=(jax.ShapeDtypeStruct((1, 1), F32), jax....  144 us

profile of v1, /device:TPU:1, one launch (start us, length us, event | category | flops | bytes accessed | tf_op | source)
XLA Modules:
  0.0 152.6 jit_solution(15759484919587611298)
XLA Ops:
  1.9 1.3 reshape.18.gain
  3.2 1.3 reshape.19.probe
  4.5 143.7 %pooled_loss.1 = (f32[1,1]{1,0:T(1,128)}, f32[4,1152]{1,0:T(4,128)}, f32[4,1152]{1,0:T(4,128)}) custom-call(bf16[1024,1152]{1,0:T(8,128)(2,1)} %patches.1, s32[4]{0:T(128)} %counts.1, s32[4]{0:T(128)} %offsets.1, f32[1,1152]{1,0:T(1,128)} %reshape.18.gain, bf16[36,4304]{1,0:T(8,128)(2,1)} %win.1, bf16[36,4304]{1,0:T(8,128)(2,1)} %bitcast.3, ...), custom_call_target="tpu_custom_call" | custom-call | flops 20308819968 | bytes 12582912 | tf_op jit(solution)/shard_map/pooled_loss/pallas_call | solution.py:564
  148.8 1.3 copy.23
  150.1 1.3 copy.24

commit v2 on v1

--- a/solution.py
+++ b/solution.py
@@ -28,10 +28,16 @@
 GROUP = 4 * BLOCK
 TILE = 256
 
-LAG_A, LAG_B, LAG_C, LAG_D, LAG_E = 1, 2, 3, 4, 5
-TICKS = CHUNKS + LAG_E
-
-Z, A_MINUS, A_PLUS, A_FAR, B_MINUS, B_PLUS, B_FAR, SIB = range(8)
+LAG_A, LAG_B, LAG_C, LAG_D, LAG_E = 2, 4, 6, 8, 9
+
+SHARED = 3
+GATHERED = CHUNKS - SHARED
+TICKS = GATHERED + LAG_E
+HANDED_TICKS = (14, 17, 20)
+TWO_AT = (15, 18, 21)
+TEXT_TICKS = (4, 7, 11, 15, 18, 21)
+
+Z, A_MINUS, A_PLUS, A_FAR, B_MINUS, B_PLUS, B_FAR, SIB, HAND = range(9)
 
 NT = (((1,), (1,)), ((), ()))
 
@@ -47,7 +53,7 @@
 def kernel(
     patches, counts, offsets, gain, win, woutt, probe, key_w, value_w, out_w, text, labels, scale, bias,
     loss_out, igrad_out, tgrad_out,
-    xbuf, normed, acc, G, a2a_s, a2a_r, compact, T, line_f, tx_s, tx_r, ix_s, ix_r, PI, tcol,
+    xbuf, normed, acc, act, G, own_blocks, a2a_s, a2a_r, compact, T, line_f, tx_s, tx_r, ix_s, ix_r, PI, tcol,
     ps_s, ps_r, ig_s, ig_r, cn_s, cn_r, hk, kw, vw, ow, ilab, tlab, ls_s, ls_r,
     loc_sem, g_ss, g_rs, x_ss, x_rs, tx_ss, tx_rs, ty_ss, ty_rs, tz_ss, tz_rs, ts_ss, ts_rs,
     ix_ss, ix_rs, iy_ss, iy_rs, ps_ss, ps_rs, ig_ss, ig_rs, cn_ss, cn_rs,
@@ -165,9 +171,7 @@
         for s in range(4):
             compact[s * SHARD:(s + 1) * SHARD, :] = a2a_r[s, 0:SHARD, :].astype(F32)
         for c in range(CHUNKS):
-            G[c, k, b, pl.ds(pl.multiple_of(a * BLOCK, 16), BLOCK), :] = compact[
-                :, c * LANES:(c + 1) * LANES
-            ].astype(BF16)
+            own_blocks[c] = compact[:, c * LANES:(c + 1) * LANES].astype(BF16)
 
     edge = jnp.logical_or(zl == 0, zl == 3)
     outward = jnp.where(zl == 3, 1, 7)
@@ -198,61 +202,101 @@
         row = jnp.broadcast_to(labels[...].astype(F32), (rows, TEXTS))
         return jnp.sum(jnp.where(lanes == ids, row, 0.0), axis=1, keepdims=True)
 
+    parity = lax.rem(zl, 2)
+    hand_to = tuple(jnp.where(k == 0, p, m) for p, m in zip(z_plus, z_minus))
+
+    def gathered(i):
+        return jnp.where(i < SHARED, 2 * i + parity, i + SHARED)
+
+    def part(c, p):
+        pieces = [G[c, 0, p]]
+        for yy in range(4):
+            pieces.append(G[c, 1, yy, p * BLOCK:(p + 1) * BLOCK, :])
+        return jnp.concatenate(pieces, axis=0)
+
+    def w1_of(c):
+        return jnp.concatenate([part(c, 0), part(c, 1)], axis=1)
+
+    def w2_of(c):
+        return jnp.concatenate([part(c, 2), part(c, 3)], axis=1)
+
     def tick(t, carry):
-        @pl.when(t < CHUNKS)
-        def _():
-            c = t
-            own = a_block(c, a)
-
-            @pl.when(jnp.logical_not(source))
+        for q in range(2):
+
+            @pl.when(2 * t + q < CHUNKS)
             def _():
-                wait_recv(own, g_rs.at[Z, c])
-
-            @pl.when(edge)
-            def _():
-                rcopy(own, own, g_ss.at[Z, c], g_rs.at[Z, c], z_to).start()
-
-            rcopy(own, own, g_ss.at[A_MINUS, c], g_rs.at[A_MINUS, c], a_plus).start()
-            rcopy(own, own, g_ss.at[A_PLUS, c], g_rs.at[A_PLUS, c], a_minus).start()
-
-        @pl.when(jnp.logical_and(t >= LAG_A, t < CHUNKS + LAG_A))
-        def _():
-            c = t - LAG_A
-            even = lax.rem(c, 2) == 0
+                c = 2 * t + q
+                own = own_blocks.at[c]
+
+                @pl.when(jnp.logical_not(source))
+                def _():
+                    wait_recv(own, g_rs.at[Z, c])
+
+                @pl.when(edge)
+                def _():
+                    rcopy(own, own, g_ss.at[Z, c], g_rs.at[Z, c], z_to).start()
+
+        @pl.when(t < GATHERED)
+        def _():
+            c = gathered(t)
+            own = own_blocks.at[c]
+            there = a_block(c, a)
+            rcopy(own, there, g_ss.at[A_MINUS, c], g_rs.at[A_MINUS, c], a_plus).start()
+            rcopy(own, there, g_ss.at[A_PLUS, c], g_rs.at[A_PLUS, c], a_minus).start()
+            there[...] = own[...]
+
+        @pl.when(jnp.logical_and(t >= LAG_A, t < GATHERED + LAG_A))
+        def _():
+            even = lax.rem(t - LAG_A, 2) == 0
+            c = gathered(t - LAG_A)
             blk = a_block(c, m4(a + jnp.where(even, 3, 1)))
             wait_recv(blk, g_rs.at[jnp.where(even, A_MINUS, A_PLUS), c])
             to = tuple(jnp.where(even, p, m) for p, m in zip(a_plus, a_minus))
             rcopy(blk, blk, g_ss.at[A_FAR, c], g_rs.at[A_FAR, c], to).start()
 
-        @pl.when(jnp.logical_and(t >= LAG_B, t < CHUNKS + LAG_B))
-        def _():
-            c = t - LAG_B
-            even = lax.rem(c, 2) == 0
+        @pl.when(jnp.logical_and(t >= LAG_C, t < GATHERED + LAG_C))
+        def _():
+            even = lax.rem(t - LAG_C, 2) == 0
+            c = gathered(t - LAG_C)
+            grp = b_group(c, m4(b + jnp.where(even, 3, 1)))
+            wait_recv(grp, g_rs.at[jnp.where(even, B_MINUS, B_PLUS), c])
+            to = tuple(jnp.where(even, p, m) for p, m in zip(b_plus, b_minus))
+            rcopy(grp, grp, g_ss.at[B_FAR, c], g_rs.at[B_FAR, c], to).start()
+
+        @pl.when(jnp.logical_and(t >= LAG_B, t < GATHERED + LAG_B))
+        def _():
+            even = lax.rem(t - LAG_B, 2) == 0
+            c = gathered(t - LAG_B)
             wait_recv(a_block(c, m4(a + jnp.where(even, 1, 3))), g_rs.at[jnp.where(even, A_PLUS, A_MINUS), c])
             wait_recv(a_block(c, m4(a + 2)), g_rs.at[A_FAR, c])
             grp = b_group(c, b)
             rcopy(grp, grp, g_ss.at[B_MINUS, c], g_rs.at[B_MINUS, c], b_plus).start()
             rcopy(grp, grp, g_ss.at[B_PLUS, c], g_rs.at[B_PLUS, c], b_minus).start()
 
-        @pl.when(jnp.logical_and(t >= LAG_C, t < CHUNKS + LAG_C))
-        def _():
-            c = t - LAG_C
-            even = lax.rem(c, 2) == 0
-            grp = b_group(c, m4(b + jnp.where(even, 3, 1)))
-            wait_recv(grp, g_rs.at[jnp.where(even, B_MINUS, B_PLUS), c])
-            to = tuple(jnp.where(even, p, m) for p, m in zip(b_plus, b_minus))
-            rcopy(grp, grp, g_ss.at[B_FAR, c], g_rs.at[B_FAR, c], to).start()
-
-        @pl.when(jnp.logical_and(t >= LAG_D, t < CHUNKS + LAG_D))
-        def _():
-            c = t - LAG_D
-            even = lax.rem(c, 2) == 0
+        @pl.when(jnp.logical_and(t >= LAG_D, t < GATHERED + LAG_D))
+        def _():
+            even = lax.rem(t - LAG_D, 2) == 0
+            i = t - LAG_D
+            c = gathered(i)
             wait_recv(b_group(c, m4(b + jnp.where(even, 1, 3))), g_rs.at[jnp.where(even, B_PLUS, B_MINUS), c])
             wait_recv(b_group(c, m4(b + 2)), g_rs.at[B_FAR, c])
             half = G.at[c, k]
             rcopy(half, half, g_ss.at[SIB, c], g_rs.at[SIB, c], sib).start()
 
-        @pl.when(t == 0)
+            @pl.when(i < SHARED)
+            def _():
+                rcopy(half, half, g_ss.at[HAND, c], g_rs.at[HAND, c], hand_to).start()
+
+        for j, at in enumerate(HANDED_TICKS):
+
+            @pl.when(t == at)
+            def _():
+                c = 2 * j + 1 - parity
+                half = G.at[c, k]
+                wait_recv(half, g_rs.at[HAND, c])
+                rcopy(half, half, g_ss.at[SIB, c], g_rs.at[SIB, c], sib).start()
+
+        @pl.when(t == TEXT_TICKS[0])
         def _():
             for i in (1, 2, 3):
                 s = m4(x + i)
@@ -262,7 +306,7 @@
             for i in (1, 2, 3):
                 rcopy(blk, blk, ty_ss.at[i - 1], ty_rs.at[y], dev(x, m4(y + i), z, k)).start()
 
-        @pl.when(t == 1)
+        @pl.when(t == TEXT_TICKS[1])
         def _():
             for i in (1, 2, 3):
                 yy = m4(y + i)
@@ -273,7 +317,7 @@
 
         for hop in (1, 2):
 
-            @pl.when(t == 1 + 2 * hop)
+            @pl.when(t == TEXT_TICKS[1 + hop])
             def _():
                 low, high = text_ring(8 - hop), text_ring(hop)
                 wait_recv(low, tz_rs.at[0, hop - 1])
@@ -281,7 +325,7 @@
                 rcopy(low, low, tz_ss.at[0, hop], tz_rs.at[0, hop], z_plus).start()
                 rcopy(high, high, tz_ss.at[1, hop], tz_rs.at[1, hop], z_minus).start()
 
-        @pl.when(t == 7)
+        @pl.when(t == TEXT_TICKS[4])
         def _():
             low, high = text_ring(5), text_ring(3)
             wait_recv(low, tz_rs.at[0, 2])
@@ -295,7 +339,7 @@
             def _():
                 rcopy(high, high, tz_ss.at[0, 3], tz_rs.at[0, 3], z_minus).start()
 
-        @pl.when(t == 9)
+        @pl.when(t == TEXT_TICKS[5])
         def _():
             wait_recv(text_ring(4), tz_rs.at[0, 3])
             mine = T.at[:, k]
@@ -314,6 +358,7 @@
             spread = jnp.mean(off * off, axis=1, keepdims=True)
             normed[sl, :] = (off * lax.rsqrt(spread + EPSILON) * gain[...]).astype(BF16)
             acc[sl, :] = wide
+            act[sl, :] = jnp.zeros((TILE, 2 * LANES), BF16)
 
         @pl.when(t == 4)
         def _():
@@ -348,31 +393,49 @@
             tid = m4(tz) * 256 + k * 128 + lax.div(tz, 4) * 64 + y * 16 + x * 4 + m4(tpos)
             tlab[...] = jnp.broadcast_to(label_cols(tid), (64, LANES))
 
-        @pl.when(t >= LAG_E)
-        def _():
-            c = t - LAG_E
-            wait_recv(G.at[c, 1 - k], g_rs.at[SIB, c])
-
-            def part(p):
-                pieces = [G[c, 0, p]]
-                for yy in range(4):
-                    pieces.append(G[c, 1, yy, p * BLOCK:(p + 1) * BLOCK, :])
-                return jnp.concatenate(pieces, axis=0)
-
-            w1 = jnp.concatenate([part(0), part(1)], axis=1)
-            w2 = jnp.concatenate([part(2), part(3)], axis=1)
-            for r in range(PACK // TILE):
-                sl = slice(r * TILE, (r + 1) * TILE)
-                hidden = jnp.dot(normed[sl, :], w1, preferred_element_type=F32)
-                acc[sl, :] += lax.dot_general(gelu(hidden), w2, NT, preferred_element_type=F32)
+        def chunk_at(u):
+            at = [tick_ - LAG_E + j + 1 for j, tick_ in enumerate(TWO_AT)]
+            later = [jnp.where(u > v, 1, 0) for v in at]
+            c = gathered(u - sum(later))
+            for j, v in enumerate(at):
+                c = jnp.where(u == v, 2 * j + 1 - parity, c)
+            return c
+
+        @pl.when(jnp.logical_and(t >= LAG_E, t < GATHERED + LAG_E))
+        def _():
+            first = t - LAG_E + sum(jnp.where(t > v, 1, 0) for v in TWO_AT)
+            many = 1 + sum(jnp.where(t == v, 1, 0) for v in TWO_AT)
+
+            def one(n, carry):
+                u = first + n
+                c = chunk_at(u)
+                before = chunk_at(jnp.maximum(u - 1, 0))
+                wait_recv(G.at[c, 1 - k], g_rs.at[SIB, c])
+                w1, w2 = w1_of(c), w2_of(before)
+                for r in range(PACK // TILE):
+                    sl = slice(r * TILE, (r + 1) * TILE)
+                    old = act[sl, :]
+                    hidden = jnp.dot(normed[sl, :], w1, preferred_element_type=F32)
+                    acc[sl, :] += lax.dot_general(old, w2, NT, preferred_element_type=F32)
+                    act[sl, :] = gelu(hidden)
+                return carry
+
+            lax.fori_loop(0, many, one, 0)
 
         return carry
 
     lax.fori_loop(0, TICKS, tick, 0)
 
     states = normed
-    states[...] = acc[...].astype(BF16)
-    scores = lax.dot_general(hk[...], states[...], NT, preferred_element_type=F32)
+    w2 = w2_of(CHUNKS - 1)
+    score_tiles = []
+    for r in range(PACK // TILE):
+        sl = slice(r * TILE, (r + 1) * TILE)
+        mixed = lax.dot_general(act[sl, :], w2, NT, preferred_element_type=F32)
+        low = (acc[sl, :] + mixed).astype(BF16)
+        states[sl, :] = low
+        score_tiles.append(lax.dot_general(hk[...], low, NT, preferred_element_type=F32))
+    scores = jnp.concatenate(score_tiles, axis=1)
     row = lax.broadcasted_iota(I32, (HEADS, PACK), 1)
     all_weights = []
     for j in range(4):
@@ -515,17 +578,26 @@
     loss_out[...] = total[0:1, 0:1] / float(TEXTS)
 
     def drain(c, carry):
-        own = a_block(c, a)
+        own = own_blocks.at[c]
 
         @pl.when(edge)
         def _():
             wait_send(own, g_ss.at[Z, c])
 
-        for kind in (A_MINUS, A_PLUS, A_FAR):
-            wait_send(own, g_ss.at[kind, c])
-        for kind in (B_MINUS, B_PLUS, B_FAR):
-            wait_send(b_group(c, b), g_ss.at[kind, c])
         wait_send(G.at[c, k], g_ss.at[SIB, c])
+
+        @pl.when(c < GATHERED)
+        def _():
+            e = gathered(c)
+            for kind in (A_MINUS, A_PLUS, A_FAR):
+                wait_send(own, g_ss.at[kind, e])
+            for kind in (B_MINUS, B_PLUS, B_FAR):
+                wait_send(b_group(e, b), g_ss.at[kind, e])
+
+            @pl.when(c < SHARED)
+            def _():
+                wait_send(G.at[e, k], g_ss.at[HAND, e])
+
         return carry
 
     lax.fori_loop(0, CHUNKS, drain, 0)
@@ -576,7 +648,9 @@
             pltpu.VMEM((PACK, D), BF16),
             pltpu.VMEM((PACK, D), BF16),
             pltpu.VMEM((PACK, D), F32),
+            pltpu.VMEM((PACK, 2 * LANES), BF16),
             pltpu.VMEM((CHUNKS, 2, 4, GROUP, LANES), BF16),
+            pltpu.VMEM((CHUNKS, BLOCK, LANES), BF16),
             pltpu.VMEM((4, SLOT_ROWS, HALF), BF16),
             pltpu.VMEM((4, SLOT_ROWS, HALF), BF16),
             pltpu.VMEM((BLOCK, HALF), F32),
@@ -603,7 +677,7 @@
             pltpu.VMEM((3, 8, LANES), F32),
             pltpu.VMEM((3, 8, 8, LANES), F32),
             dma((5,)),
-            dma((8, CHUNKS)), dma((8, CHUNKS)),
+            dma((9, CHUNKS)), dma((9, CHUNKS)),
             dma((3,)), dma((4,)),
             dma((3,)), dma((4,)),
             dma((3,)), dma((4,)),

time: 153 us -> 130 us (0.85)
  Pallas kernels: 144 us -> 121 us
    pallas_call x1, Pallas kernels: 144 us -> 121 us  [per_device(): pl.pallas_call(kernel, out_shape=(jax.ShapeDtypeStruct((1, 1), F32), jax....]
where the time goes in v2:
time: 130 us
  Pallas kernels  121 us (93%)
  local copies, waits for them, and re-layouts  5.23 us (4%)
  between operations  3.68 us (3%)
    pallas_call x1, Pallas kernels, per_device(): pl.pallas_call(kernel, out_shape=(jax.ShapeDtypeStruct((1, 1), F32), jax....  121 us
    unnamed x2, local copies, waits for them, and re-layouts  2.66 us

profile of v2, /device:TPU:1, one launch (start us, length us, event | category | flops | bytes accessed | tf_op | source)
XLA Modules:
  0.0 129.9 jit_solution(4751448430005307746)
XLA Ops:
  1.9 1.3 reshape.18.gain
  3.2 1.3 reshape.19.probe
  4.5 121.0 %pooled_loss.1 = (f32[1,1]{1,0:T(1,128)}, f32[4,1152]{1,0:T(4,128)}, f32[4,1152]{1,0:T(4,128)}) custom-call(bf16[1024,1152]{1,0:T(8,128)(2,1)} %patches.1, s32[4]{0:T(128)} %counts.1, s32[4]{0:T(128)} %offsets.1, f32[1,1152]{1,0:T(1,128)} %reshape.18.gain, bf16[36,4304]{1,0:T(8,128)(2,1)} %win.1, bf16[36,4304]{1,0:T(8,128)(2,1)} %bitcast.3, ...), custom_call_target="tpu_custom_call" | custom-call | flops 20308819968 | bytes 12582912 | tf_op jit(solution)/shard_map/pooled_loss/pallas_call | solution.py:636
  126.1 1.3 %copy.23 = f32[4,1152]{1,0:T(4,128)} copy(f32[4,1152]{1,0:T(4,128)} %get-tuple-element.13) | data formatting | bytes 36864
  127.5 1.3 %copy.24 = f32[4,1152]{1,0:T(4,128)} copy(f32[4,1152]{1,0:T(4,128)} %get-tuple-element.14) | data formatting | bytes 36864

commit v3 on v2

--- a/solution.py
+++ b/solution.py
@@ -35,7 +35,9 @@
 TICKS = GATHERED + LAG_E
 HANDED_TICKS = (14, 17, 20)
 TWO_AT = (15, 18, 21)
-TEXT_TICKS = (4, 7, 11, 15, 18, 21)
+TEXT_TICKS = (3, 6, 9, 12, 15, 18)
+PIECES = ((0, 4), (4, 10), (10, 17))
+PIECE_TICKS = (1, 4)
 
 Z, A_MINUS, A_PLUS, A_FAR, B_MINUS, B_PLUS, B_FAR, SIB, HAND = range(9)
 
@@ -51,9 +53,9 @@
 
 
 def kernel(
-    patches, counts, offsets, gain, win, woutt, probe, key_w, value_w, out_w, text, labels, scale, bias,
+    patches, counts, offsets, gain, win_hbm, woutt_hbm, probe, key_w, value_w, out_w, text, labels, scale, bias,
     loss_out, igrad_out, tgrad_out,
-    xbuf, normed, acc, act, G, own_blocks, a2a_s, a2a_r, compact, T, line_f, tx_s, tx_r, ix_s, ix_r, PI, tcol,
+    xbuf, normed, acc, act, G, own_blocks, win, woutt, a2a_s, a2a_r, compact, T, line_f, tx_s, tx_r, ix_s, ix_r, line_i, PI, tcol,
     ps_s, ps_r, ig_s, ig_r, cn_s, cn_r, hk, kw, vw, ow, ilab, tlab, ls_s, ls_r,
     loc_sem, g_ss, g_rs, x_ss, x_rs, tx_ss, tx_rs, ty_ss, ty_rs, tz_ss, tz_rs, ts_ss, ts_rs,
     ix_ss, ix_rs, iy_ss, iy_rs, ps_ss, ps_rs, ig_ss, ig_rs, cn_ss, cn_rs,
@@ -93,6 +95,19 @@
     def wait_send(ref, ss):
         rcopy(ref, ref, ss, loc_sem.at[0], sib).wait_send()
 
+    shards = [
+        pltpu.make_async_copy(win_hbm, win, loc_sem.at[5]),
+        pltpu.make_async_copy(woutt_hbm, woutt, loc_sem.at[6]),
+    ]
+    for cp in shards:
+        cp.start()
+    local = [
+        pltpu.make_async_copy(patches, xbuf, loc_sem.at[1]),
+        pltpu.make_async_copy(key_w, kw, loc_sem.at[2]),
+        pltpu.make_async_copy(value_w, vw, loc_sem.at[3]),
+        pltpu.make_async_copy(out_w, ow, loc_sem.at[4]),
+    ]
+
     barrier = pltpu.get_barrier_semaphore()
     partners = list(xs) + list(zs) + [sib]
     for i in (1, 2, 3):
@@ -102,14 +117,9 @@
     for p in partners:
         pl.semaphore_signal(barrier, inc=1, device_id=p, device_id_type=MESH)
 
-    local = [
-        pltpu.make_async_copy(patches, xbuf, loc_sem.at[1]),
-        pltpu.make_async_copy(key_w, kw, loc_sem.at[2]),
-        pltpu.make_async_copy(value_w, vw, loc_sem.at[3]),
-        pltpu.make_async_copy(out_w, ow, loc_sem.at[4]),
-    ]
-    for cp in local:
-        cp.start()
+    for cp in shards:
+        cp.wait()
+    local[0].start()
 
     source = k == zh
 
@@ -133,11 +143,18 @@
 
     pl.semaphore_wait(barrier, len(partners))
 
+    def piece_lanes(p):
+        return slice(PIECES[p][0] * LANES, PIECES[p][1] * LANES)
+
     @pl.when(source)
     def _():
-        for i in range(3):
-            to_x = m4(x + i + 1)
-            rcopy(a2a_s.at[to_x], a2a_r.at[x], x_ss.at[i], x_rs.at[x], xs[i]).start()
+        for p in range(len(PIECES)):
+            at = piece_lanes(p)
+            for i in range(3):
+                to_x = m4(x + i + 1)
+                rcopy(
+                    a2a_s.at[to_x, :, at], a2a_r.at[x, :, at], x_ss.at[p, i], x_rs.at[p, x], xs[i]
+                ).start()
         a2a_r[x] = a2a_s[x]
 
     for i in range(3):
@@ -163,15 +180,19 @@
     def b_group(c, at):
         return G.at[c, k, at]
 
+    def take_piece(p):
+        at = piece_lanes(p)
+        for i in (1, 2, 3):
+            s = m4(x + i)
+            wait_recv(a2a_r.at[s, :, at], x_rs.at[p, s])
+        for s in range(4):
+            compact[s * SHARD:(s + 1) * SHARD, at] = a2a_r[s, 0:SHARD, at].astype(F32)
+        for c in range(*PIECES[p]):
+            own_blocks[c] = compact[:, c * LANES:(c + 1) * LANES].astype(BF16)
+
     @pl.when(source)
     def _():
-        for i in (1, 2, 3):
-            s = m4(x + i)
-            wait_recv(a2a_r.at[s], x_rs.at[s])
-        for s in range(4):
-            compact[s * SHARD:(s + 1) * SHARD, :] = a2a_r[s, 0:SHARD, :].astype(F32)
-        for c in range(CHUNKS):
-            own_blocks[c] = compact[:, c * LANES:(c + 1) * LANES].astype(BF16)
+        take_piece(0)
 
     edge = jnp.logical_or(zl == 0, zl == 3)
     outward = jnp.where(zl == 3, 1, 7)
@@ -221,6 +242,12 @@
         return jnp.concatenate([part(c, 2), part(c, 3)], axis=1)
 
     def tick(t, carry):
+        for p, at in enumerate(PIECE_TICKS):
+
+            @pl.when(jnp.logical_and(source, t == at))
+            def _():
+                take_piece(p + 1)
+
         for q in range(2):
 
             @pl.when(2 * t + q < CHUNKS)
@@ -345,27 +372,46 @@
             mine = T.at[:, k]
             rcopy(mine, mine, ts_ss.at[0], ts_rs.at[0], sib).start()
 
+        @pl.when(t == TEXT_TICKS[5] + 1)
+        def _():
+            for zz in range(8):
+                block = T[zz % 4, k, zz // 4, own_t, :].astype(F32)
+                mine = jnp.zeros((4, D), F32)
+                for s in range(4):
+                    mine = mine + jnp.where(x == s, 1.0, 0.0) * block[4 * s:4 * s + 4, :]
+                tcol[8 * zz:8 * zz + 4, :] = mine
+                tcol[8 * zz + 4:8 * zz + 8, :] = jnp.zeros((4, D), F32)
+
         @pl.when(t == 0)
         def _():
+            local[1].start()
+
+        @pl.when(t == 1)
+        def _():
             local[0].wait()
 
-        @pl.when(t < PACK // TILE)
-        def _():
-            sl = pl.ds(pl.multiple_of(t * TILE, TILE), TILE)
+        @pl.when(t == 8)
+        def _():
+            local[2].start()
+            local[3].start()
+
+        @pl.when(jnp.logical_and(t >= 1, t <= PACK // TILE))
+        def _():
+            sl = pl.ds(pl.multiple_of((t - 1) * TILE, TILE), TILE)
             wide = xbuf[sl, :].astype(F32)
             center = jnp.mean(wide, axis=1, keepdims=True)
             off = wide - center
             spread = jnp.mean(off * off, axis=1, keepdims=True)
-            normed[sl, :] = (off * lax.rsqrt(spread + EPSILON) * gain[...]).astype(BF16)
+            normed[sl, :] = (off * lax.rsqrt(spread + EPSILON) * gain[...].reshape(1, D)).astype(BF16)
             acc[sl, :] = wide
             act[sl, :] = jnp.zeros((TILE, 2 * LANES), BF16)
 
-        @pl.when(t == 4)
+        @pl.when(t == 7)
         def _():
             local[1].wait()
             head_of = lax.div(lax.broadcasted_iota(I32, (HEADS, D), 1), HEAD_DIM)
             own_head = head_of == lax.broadcasted_iota(I32, (HEADS, D), 0)
-            block = jnp.where(own_head, jnp.broadcast_to(probe[...].astype(F32), (HEADS, D)), 0.0)
+            block = jnp.where(own_head, jnp.broadcast_to(probe[...].astype(F32).reshape(1, D), (HEADS, D)), 0.0)
             keys = lax.dot_general(block.astype(BF16), kw[...], NT, preferred_element_type=F32)
             hk[...] = (keys / math.sqrt(HEAD_DIM)).astype(BF16)
 
@@ -463,7 +509,8 @@
     pooled = jnp.dot(mixed, ow[...], preferred_element_type=F32)[0:8, :]
     image_inv = lax.rsqrt(jnp.sum(pooled * pooled, axis=1, keepdims=True) + EPSILON)
     image_unit = pooled * image_inv
-    ix_s[...] = jnp.concatenate([image_unit, jnp.zeros((8, D), F32)], axis=0).astype(BF16)
+    image_low = jnp.concatenate([image_unit, jnp.zeros((8, D), F32)], axis=0).astype(BF16)
+    ix_s[...] = image_low[0:8].astype(F32)[0:4]
 
     for i in range(3):
         rcopy(ix_s, ix_r.at[x], ix_ss.at[i], ix_rs.at[x], xs[i]).start()
@@ -474,7 +521,7 @@
 
     wait_recv(T.at[:, 1 - k], ts_rs.at[0])
     texts = T[...].reshape(TEXTS, D)
-    own_logits = mult * lax.dot_general(ix_s[...], texts, NT, preferred_element_type=F32) + shift
+    own_logits = mult * lax.dot_general(image_low, texts, NT, preferred_element_type=F32) + shift
     slot = lax.broadcasted_iota(I32, (16, 1), 0)
     slot4 = m4(slot)
     own_ids = 4 * (g * 32 + lax.rem(d + 32 - 8 * slot4, 32)) + slot4
@@ -492,7 +539,9 @@
     for i in (1, 2, 3):
         s = m4(x + i)
         wait_recv(ix_r.at[s], ix_rs.at[s])
-    PI[k, own_t, :] = gather_line(ix_r, line_f)
+    for s in range(4):
+        line_i[4 * s:4 * s + 4, :] = ix_r[s]
+    PI[k, own_t, :] = line_i[...].astype(BF16)
     others = [(m4(y + i), c_) for i in (1, 2, 3) for c_ in (0, 1)]
     to_plane = [dev(x, yy, z, c_) for yy, c_ in others] + [sib]
     blk = PI.at[k, own_t, :]
@@ -519,14 +568,6 @@
         rcopy(ig_s.at[j], ig_r.at[j], ig_ss.at[j], ig_rs.at[j], group_dev[4 - j]).start()
     ig_r[0] = ig_s[0]
 
-    for zz in range(8):
-        block = T[zz % 4, k, zz // 4, own_t, :].astype(F32)
-        mine = jnp.zeros((4, D), F32)
-        for s in range(4):
-            mine = mine + jnp.where(x == s, 1.0, 0.0) * block[4 * s:4 * s + 4, :]
-        tcol[8 * zz:8 * zz + 4, :] = mine
-        tcol[8 * zz + 4:8 * zz + 8, :] = jnp.zeros((4, D), F32)
-
     for yy, c_ in others + [(y, 1 - k)]:
         wait_recv(PI.at[c_, pl.ds(pl.multiple_of(yy * 16, 16), 16), :], iy_rs.at[c_, yy])
     plane = PI[...].reshape(LANES, D)
@@ -537,7 +578,7 @@
     plane_slope = (mult * -plane_sign * jax.nn.sigmoid(-plane_sign * plane_logits)).astype(BF16)
     push = jnp.dot(plane_slope, plane, preferred_element_type=F32)
     for zz in range(8):
-        ps_s[zz] = push[8 * zz:8 * zz + 8, :]
+        ps_s[zz] = push[8 * zz:8 * zz + 4, :]
     for i in range(7):
         to_z = m8(z + i + 1)
         rcopy(ps_s.at[to_z], ps_r.at[z], ps_ss.at[i], ps_rs.at[z], zs[i]).start()
@@ -558,25 +599,6 @@
     for j in range(4):
         igrad_out[j:j + 1, :] = ig_r[j]
 
-    for i in range(1, 8):
-        zz = m8(z + i)
-        wait_recv(ps_r.at[zz], ps_rs.at[zz])
-    text_push = ps_r[0]
-    for i in range(1, 8):
-        text_push = text_push + ps_r[i]
-    text_push = text_push[0:4, :]
-    tgrad_out[...] = (
-        text_push - text_unit * jnp.sum(text_unit * text_push, axis=1, keepdims=True)
-    ) * text_inv
-
-    for i in range(1, 8):
-        zz = m8(z + i)
-        wait_recv(ls_r.at[2, zz], l3_rs.at[zz])
-    total = ls_r[2, 0]
-    for i in range(1, 8):
-        total = total + ls_r[2, i]
-    loss_out[...] = total[0:1, 0:1] / float(TEXTS)
-
     def drain(c, carry):
         own = own_blocks.at[c]
 
@@ -604,8 +626,9 @@
 
     @pl.when(source)
     def _():
-        for i in range(3):
-            wait_send(a2a_s.at[0], x_ss.at[i])
+        for p in range(len(PIECES)):
+            for i in range(3):
+                wait_send(a2a_s.at[0, :, piece_lanes(p)], x_ss.at[p, i])
 
     for i in range(3):
         wait_send(tx_s, tx_ss.at[i])
@@ -618,6 +641,24 @@
         wait_send(text_ring(0), tz_ss.at[1, i])
     wait_send(text_ring(0), tz_ss.at[0, 3])
     wait_send(T.at[:, k], ts_ss.at[0])
+    for i in range(1, 8):
+        zz = m8(z + i)
+        wait_recv(ps_r.at[zz], ps_rs.at[zz])
+    text_push = ps_r[0]
+    for i in range(1, 8):
+        text_push = text_push + ps_r[i]
+    tgrad_out[...] = (
+        text_push - text_unit * jnp.sum(text_unit * text_push, axis=1, keepdims=True)
+    ) * text_inv
+
+    for i in range(1, 8):
+        zz = m8(z + i)
+        wait_recv(ls_r.at[2, zz], l3_rs.at[zz])
+    total = ls_r[2, 0]
+    for i in range(1, 8):
+        total = total + ls_r[2, i]
+    loss_out[...] = total[0:1, 0:1] / float(TEXTS)
+
     for i in range(7):
         wait_send(PI.at[k, own_t, :], iy_ss.at[i])
         wait_send(ls_s.at[1], l2_ss.at[i])
@@ -641,7 +682,7 @@
             jax.ShapeDtypeStruct((4, D), F32),
         ),
         in_specs=[
-            anywhere, smem, smem, vmem, vmem, vmem, vmem, anywhere, anywhere, anywhere, vmem, vmem, smem, smem,
+            anywhere, smem, smem, vmem, anywhere, anywhere, vmem, anywhere, anywhere, anywhere, vmem, vmem, smem, smem,
         ],
         out_specs=(vmem, vmem, vmem),
         scratch_shapes=[
@@ -651,6 +692,8 @@
             pltpu.VMEM((PACK, 2 * LANES), BF16),
             pltpu.VMEM((CHUNKS, 2, 4, GROUP, LANES), BF16),
             pltpu.VMEM((CHUNKS, BLOCK, LANES), BF16),
+            pltpu.VMEM((SHARD, FF), BF16),
+            pltpu.VMEM((SHARD, FF), BF16),
             pltpu.VMEM((4, SLOT_ROWS, HALF), BF16),
             pltpu.VMEM((4, SLOT_ROWS, HALF), BF16),
             pltpu.VMEM((BLOCK, HALF), F32),
@@ -658,12 +701,13 @@
             pltpu.VMEM((16, D), F32),
             pltpu.VMEM((16, D), BF16),
             pltpu.VMEM((4, 16, D), BF16),
-            pltpu.VMEM((16, D), BF16),
-            pltpu.VMEM((4, 16, D), BF16),
+            pltpu.VMEM((4, D), F32),
+            pltpu.VMEM((4, 4, D), F32),
+            pltpu.VMEM((16, D), F32),
             pltpu.VMEM((2, 64, D), BF16),
             pltpu.VMEM((64, D), F32),
-            pltpu.VMEM((8, 8, D), F32),
-            pltpu.VMEM((8, 8, D), F32),
+            pltpu.VMEM((8, 4, D), F32),
+            pltpu.VMEM((8, 4, D), F32),
             pltpu.VMEM((4, 1, D), F32),
             pltpu.VMEM((4, 1, D), F32),
             pltpu.VMEM((4, 8, LANES), I32),
@@ -676,9 +720,9 @@
             pltpu.VMEM((64, LANES), F32),
             pltpu.VMEM((3, 8, LANES), F32),
             pltpu.VMEM((3, 8, 8, LANES), F32),
-            dma((5,)),
+            dma((7,)),
             dma((9, CHUNKS)), dma((9, CHUNKS)),
-            dma((3,)), dma((4,)),
+            dma((3, 3)), dma((3, 4)),
             dma((3,)), dma((4,)),
             dma((3,)), dma((4,)),
             dma((2, 4)), dma((2, 4)),
@@ -700,8 +744,8 @@
         ),
         name="pooled_loss",
     )(
-        patches, patch_counts, pack_offsets, norm_gain.reshape(1, D), mlp_in, mlp_out.T,
-        probe_query.reshape(1, D), key_weight, value_weight, out_weight, text_embed,
+        patches, patch_counts, pack_offsets, norm_gain, mlp_in, mlp_out.T,
+        probe_query, key_weight, value_weight, out_weight, text_embed,
         pair_label.reshape(1, TEXTS), logit_scale, logit_bias,
     )
     return loss.reshape(()), image_grad, text_grad

time: 130 us -> 120 us (0.923)
  Pallas kernels: 121 us -> 113 us
  local copies, waits for them, and re-layouts: 5.23 us -> 2.66 us
    pallas_call x1, Pallas kernels: 121 us -> 113 us  [per_device(): pl.pallas_call(kernel, out_shape=(jax.ShapeDtypeStruct((1, 1), F32), jax....]
    reshape x2 -> x0, local copies, waits for them, and re-layouts: 2.58 us -> none  [the longest x1 1.29 us: per_device(): norm_gain.reshape(1, D)]
where the time goes in v3:
time: 120 us
  Pallas kernels  113 us (94%)
  between operations  3.68 us (3%)
  local copies, waits for them, and re-layouts  2.66 us (2%)
    pallas_call x1, Pallas kernels, per_device(): pl.pallas_call(kernel, out_shape=(jax.ShapeDtypeStruct((1, 1), F32), jax....  113 us
    unnamed x2, local copies, waits for them, and re-layouts  2.66 us

profile of v3, /device:TPU:1, one launch (start us, length us, event | category | flops | bytes accessed | tf_op | source)
XLA Modules:
  0.0 119.7 jit_solution(12140220299923751767)
XLA Ops:
  1.9 113.3 %pooled_loss.1 = (f32[1,1]{1,0:T(1,128)}, f32[4,1152]{1,0:T(4,128)}, f32[4,1152]{1,0:T(4,128)}) custom-call(bf16[1024,1152]{1,0:T(8,128)(2,1)} %patches.1, s32[4]{0:T(128)} %counts.1, s32[4]{0:T(128)} %offsets.1, f32[1152]{0:T(1024)} %gain.1, bf16[36,4304]{1,0:T(8,128)(2,1)} %win_hbm.1, bf16[36,4304]{1,0:T(8,128)(2,1)} %bitcast.3, bf16[1152]{0:T(1024)(128)(2,1)} %probe.1, ...), custom_call_target="tpu_custom_call" | custom-call | flops 20308819968 | bytes 12582912 | tf_op jit(solution)/shard_map/pooled_loss/pallas_call | solution.py:677
  115.9 1.3 %copy.23 = f32[4,1152]{1,0:T(4,128)} copy(f32[4,1152]{1,0:T(4,128)} %get-tuple-element.13) | data formatting | bytes 36864
  117.2 1.3 %copy.24 = f32[4,1152]{1,0:T(4,128)} copy(f32[4,1152]{1,0:T(4,128)} %get-tuple-element.14) | data formatting | bytes 36864

commit v4 on v3

--- a/solution.py
+++ b/solution.py
@@ -27,15 +27,16 @@
 BLOCK = 4 * SHARD
 GROUP = 4 * BLOCK
 TILE = 256
-
-LAG_A, LAG_B, LAG_C, LAG_D, LAG_E = 2, 4, 6, 8, 9
+PLANE = 32
+
+LAG_A, LAG_B, LAG_C, LAG_D, LAG_E = 3, 6, 9, 12, 13
 
 SHARED = 3
 GATHERED = CHUNKS - SHARED
 TICKS = GATHERED + LAG_E
-HANDED_TICKS = (14, 17, 20)
-TWO_AT = (15, 18, 21)
-TEXT_TICKS = (3, 6, 9, 12, 15, 18)
+HANDED_TICKS = (18, 21, 24)
+TWO_AT = (19, 22, 25)
+TEXT_TICKS = (5, 9, 13, 17, 21, 24)
 PIECES = ((0, 4), (4, 10), (10, 17))
 PIECE_TICKS = (1, 4)
 
@@ -54,11 +55,11 @@
 
 def kernel(
     patches, counts, offsets, gain, win_hbm, woutt_hbm, probe, key_w, value_w, out_w, text, labels, scale, bias,
-    loss_out, igrad_out, tgrad_out,
-    xbuf, normed, acc, act, G, own_blocks, win, woutt, a2a_s, a2a_r, compact, T, line_f, tx_s, tx_r, ix_s, ix_r, line_i, PI, tcol,
+    loss_out, grads_out,
+    xbuf, normed, acc, act, G, own_blocks, win, woutt, a2a_s, a2a_r, compact, T, line_f, tx_s, tx_r, ix_s, ix_r, plane_f, tcol,
     ps_s, ps_r, ig_s, ig_r, cn_s, cn_r, hk, kw, vw, ow, ilab, tlab, ls_s, ls_r,
     loc_sem, g_ss, g_rs, x_ss, x_rs, tx_ss, tx_rs, ty_ss, ty_rs, tz_ss, tz_rs, ts_ss, ts_rs,
-    ix_ss, ix_rs, iy_ss, iy_rs, ps_ss, ps_rs, ig_ss, ig_rs, cn_ss, cn_rs,
+    ix_ss, ix_rs, ps_ss, ps_rs, ig_ss, ig_rs, cn_ss, cn_rs,
     l1_ss, l1_rs, l2_ss, l2_rs, l3_ss, l3_rs,
 ):
     g = lax.axis_index("grp")
@@ -109,11 +110,18 @@
     ]
 
     barrier = pltpu.get_barrier_semaphore()
-    partners = list(xs) + list(zs) + [sib]
-    for i in (1, 2, 3):
-        for c_ in (0, 1):
-            partners.append(dev(x, m4(y + i), z, c_))
-    partners.append(dev(x, m4(y + 2), m8(z + 4), k))
+    place = k * 16 + y * 4 + x
+
+    def in_plane(q):
+        return dev(m4(q), m4(lax.div(q, 4)), z, lax.div(q, 16))
+
+    def greet(i, carry):
+        q = lax.rem(place + i, PLANE)
+        pl.semaphore_signal(barrier, inc=1, device_id=in_plane(q), device_id_type=MESH)
+        return carry
+
+    lax.fori_loop(1, PLANE, greet, 0)
+    partners = list(zs) + [dev(x, m4(y + 2), m8(z + 4), k)]
     for p in partners:
         pl.semaphore_signal(barrier, inc=1, device_id=p, device_id_type=MESH)
 
@@ -141,7 +149,7 @@
     for j in range(4):
         cn_s[j] = jnp.full((8, LANES), counts[j], I32)
 
-    pl.semaphore_wait(barrier, len(partners))
+    pl.semaphore_wait(barrier, PLANE - 1 + len(partners))
 
     def piece_lanes(p):
         return slice(PIECES[p][0] * LANES, PIECES[p][1] * LANES)
@@ -240,6 +248,14 @@
 
     def w2_of(c):
         return jnp.concatenate([part(c, 2), part(c, 3)], axis=1)
+
+    def chunk_at(u):
+        at = [tick_ - LAG_E + j + 1 for j, tick_ in enumerate(TWO_AT)]
+        later = [jnp.where(u > v, 1, 0) for v in at]
+        c = gathered(u - sum(later))
+        for j, v in enumerate(at):
+            c = jnp.where(u == v, 2 * j + 1 - parity, c)
+        return c
 
     def tick(t, carry):
         for p, at in enumerate(PIECE_TICKS):
@@ -439,14 +455,6 @@
             tid = m4(tz) * 256 + k * 128 + lax.div(tz, 4) * 64 + y * 16 + x * 4 + m4(tpos)
             tlab[...] = jnp.broadcast_to(label_cols(tid), (64, LANES))
 
-        def chunk_at(u):
-            at = [tick_ - LAG_E + j + 1 for j, tick_ in enumerate(TWO_AT)]
-            later = [jnp.where(u > v, 1, 0) for v in at]
-            c = gathered(u - sum(later))
-            for j, v in enumerate(at):
-                c = jnp.where(u == v, 2 * j + 1 - parity, c)
-            return c
-
         @pl.when(jnp.logical_and(t >= LAG_E, t < GATHERED + LAG_E))
         def _():
             first = t - LAG_E + sum(jnp.where(t > v, 1, 0) for v in TWO_AT)
@@ -473,7 +481,7 @@
     lax.fori_loop(0, TICKS, tick, 0)
 
     states = normed
-    w2 = w2_of(CHUNKS - 1)
+    w2 = w2_of(chunk_at(CHUNKS - 1))
     score_tiles = []
     for r in range(PACK // TILE):
         sl = slice(r * TILE, (r + 1) * TILE)
@@ -510,11 +518,15 @@
     image_inv = lax.rsqrt(jnp.sum(pooled * pooled, axis=1, keepdims=True) + EPSILON)
     image_unit = pooled * image_inv
     image_low = jnp.concatenate([image_unit, jnp.zeros((8, D), F32)], axis=0).astype(BF16)
-    ix_s[...] = image_low[0:8].astype(F32)[0:4]
-
-    for i in range(3):
-        rcopy(ix_s, ix_r.at[x], ix_ss.at[i], ix_rs.at[x], xs[i]).start()
-    ix_r[x] = ix_s[...]
+    ix_s[...] = image_unit[0:4].astype(BF16)
+
+    def send_images(i, carry):
+        q = lax.rem(place + i, PLANE)
+        rcopy(ix_s, ix_r.at[place], ix_ss.at[i], ix_rs.at[place], in_plane(q)).start()
+        return carry
+
+    lax.fori_loop(1, PLANE, send_images, 0)
+    ix_r[place] = ix_s[...]
 
     mult = scale[0]
     shift = bias[0]
@@ -536,26 +548,8 @@
         rcopy(ls_s.at[0], ls_r.at[0, x], l1_ss.at[i], l1_rs.at[x], xs[i]).start()
     ls_r[0, x] = ls_s[0]
 
-    for i in (1, 2, 3):
-        s = m4(x + i)
-        wait_recv(ix_r.at[s], ix_rs.at[s])
-    for s in range(4):
-        line_i[4 * s:4 * s + 4, :] = ix_r[s]
-    PI[k, own_t, :] = line_i[...].astype(BF16)
     others = [(m4(y + i), c_) for i in (1, 2, 3) for c_ in (0, 1)]
     to_plane = [dev(x, yy, z, c_) for yy, c_ in others] + [sib]
-    blk = PI.at[k, own_t, :]
-    for i, to in enumerate(to_plane):
-        rcopy(blk, blk, iy_ss.at[i], iy_rs.at[k, y], to).start()
-
-    for i in (1, 2, 3):
-        s = m4(x + i)
-        wait_recv(ls_r.at[0, s], l1_rs.at[s])
-    ls_s[1] = ls_r[0, 0] + ls_r[0, 1] + ls_r[0, 2] + ls_r[0, 3]
-    me8 = k * 4 + y
-    for i, to in enumerate(to_plane):
-        rcopy(ls_s.at[1], ls_r.at[1, me8], l2_ss.at[i], l2_rs.at[me8], to).start()
-    ls_r[1, me8] = ls_s[1]
 
     own_slope = (mult * -sign * jax.nn.sigmoid(-signed)).astype(BF16)
     image_push = jnp.dot(own_slope, texts, preferred_element_type=F32)[0:8, :]
@@ -568,9 +562,24 @@
         rcopy(ig_s.at[j], ig_r.at[j], ig_ss.at[j], ig_rs.at[j], group_dev[4 - j]).start()
     ig_r[0] = ig_s[0]
 
-    for yy, c_ in others + [(y, 1 - k)]:
-        wait_recv(PI.at[c_, pl.ds(pl.multiple_of(yy * 16, 16), 16), :], iy_rs.at[c_, yy])
-    plane = PI[...].reshape(LANES, D)
+    for i in (1, 2, 3):
+        s = m4(x + i)
+        wait_recv(ls_r.at[0, s], l1_rs.at[s])
+    ls_s[1] = ls_r[0, 0] + ls_r[0, 1] + ls_r[0, 2] + ls_r[0, 3]
+    me8 = k * 4 + y
+    for i, to in enumerate(to_plane):
+        rcopy(ls_s.at[1], ls_r.at[1, me8], l2_ss.at[i], l2_rs.at[me8], to).start()
+    ls_r[1, me8] = ls_s[1]
+
+    def take_images(i, carry):
+        q = lax.rem(place + i, PLANE)
+        wait_recv(ix_r.at[q], ix_rs.at[q])
+        return carry
+
+    lax.fori_loop(1, PLANE, take_images, 0)
+    for q in range(PLANE):
+        plane_f[4 * q:4 * q + 4, :] = ix_r[q].astype(F32)
+    plane = plane_f[...].astype(BF16)
     plane_logits = mult * lax.dot_general(
         tcol[...].astype(BF16), plane, NT, preferred_element_type=F32
     ) + shift
@@ -597,7 +606,7 @@
     for j in (1, 2, 3):
         wait_recv(ig_r.at[j], ig_rs.at[j])
     for j in range(4):
-        igrad_out[j:j + 1, :] = ig_r[j]
+        grads_out[j:j + 1, :] = ig_r[j]
 
     def drain(c, carry):
         own = own_blocks.at[c]
@@ -633,7 +642,6 @@
     for i in range(3):
         wait_send(tx_s, tx_ss.at[i])
         wait_send(T.at[zl, k, zh, own_t, :], ty_ss.at[i])
-        wait_send(ix_s, ix_ss.at[i])
         wait_send(ls_s.at[0], l1_ss.at[i])
         wait_send(cn_s.at[i + 1], cn_ss.at[i + 1])
         wait_send(ig_s.at[i + 1], ig_ss.at[i + 1])
@@ -647,7 +655,7 @@
     text_push = ps_r[0]
     for i in range(1, 8):
         text_push = text_push + ps_r[i]
-    tgrad_out[...] = (
+    grads_out[4:8, :] = (
         text_push - text_unit * jnp.sum(text_unit * text_push, axis=1, keepdims=True)
     ) * text_inv
 
@@ -659,8 +667,12 @@
         total = total + ls_r[2, i]
     loss_out[...] = total[0:1, 0:1] / float(TEXTS)
 
+    def sent_images(i, carry):
+        wait_send(ix_s, ix_ss.at[i])
+        return carry
+
+    lax.fori_loop(1, PLANE, sent_images, 0)
     for i in range(7):
-        wait_send(PI.at[k, own_t, :], iy_ss.at[i])
         wait_send(ls_s.at[1], l2_ss.at[i])
         wait_send(ps_s.at[0], ps_ss.at[i])
         wait_send(ls_s.at[2], l3_ss.at[i])
@@ -674,17 +686,16 @@
     smem = pl.BlockSpec(memory_space=pltpu.SMEM)
     anywhere = pl.BlockSpec(memory_space=pl.ANY)
     dma = pltpu.SemaphoreType.DMA
-    loss, image_grad, text_grad = pl.pallas_call(
+    loss, grads = pl.pallas_call(
         kernel,
         out_shape=(
             jax.ShapeDtypeStruct((1, 1), F32),
-            jax.ShapeDtypeStruct((4, D), F32),
-            jax.ShapeDtypeStruct((4, D), F32),
+            jax.ShapeDtypeStruct((8, D), F32),
         ),
         in_specs=[
             anywhere, smem, smem, vmem, anywhere, anywhere, vmem, anywhere, anywhere, anywhere, vmem, vmem, smem, smem,
         ],
-        out_specs=(vmem, vmem, vmem),
+        out_specs=(vmem, vmem),
         scratch_shapes=[
             pltpu.VMEM((PACK, D), BF16),
             pltpu.VMEM((PACK, D), BF16),
@@ -701,10 +712,9 @@
             pltpu.VMEM((16, D), F32),
             pltpu.VMEM((16, D), BF16),
             pltpu.VMEM((4, 16, D), BF16),
-            pltpu.VMEM((4, D), F32),
-            pltpu.VMEM((4, 4, D), F32),
-            pltpu.VMEM((16, D), F32),
-            pltpu.VMEM((2, 64, D), BF16),
+            pltpu.VMEM((4, D), BF16),
+            pltpu.VMEM((PLANE, 4, D), BF16),
+            pltpu.VMEM((LANES, D), F32),
             pltpu.VMEM((64, D), F32),
             pltpu.VMEM((8, 4, D), F32),
             pltpu.VMEM((8, 4, D), F32),
@@ -727,8 +737,7 @@
             dma((3,)), dma((4,)),
             dma((2, 4)), dma((2, 4)),
             dma((1,)), dma((1,)),
-            dma((3,)), dma((4,)),
-            dma((7,)), dma((2, 4)),
+            dma((PLANE,)), dma((PLANE,)),
             dma((7,)), dma((8,)),
             dma((4,)), dma((4,)),
             dma((4,)), dma((4,)),
@@ -748,7 +757,7 @@
         probe_query, key_weight, value_weight, out_weight, text_embed,
         pair_label.reshape(1, TEXTS), logit_scale, logit_bias,
     )
-    return loss.reshape(()), image_grad, text_grad
+    return loss.reshape(()), grads[0:4], grads[4:8]
 
 
 def solution(mesh):

time: 120 us -> 111 us (0.925)
  Pallas kernels: 113 us -> 106 us
  local copies, waits for them, and re-layouts: 2.66 us -> 1.46 us
    pallas_call x1, Pallas kernels: 113 us -> 106 us  [per_device(): pl.pallas_call(kernel, out_shape=(jax.ShapeDtypeStruct((1, 1), F32), jax....]
    unnamed x2 -> x0, local copies, waits for them, and re-layouts: 2.66 us -> none
    slice x0 -> x1, local copies, waits for them, and re-layouts: none -> 1.46 us  [per_device(): return (loss.reshape(()), grads[0:4], grads[4:8])]
where the time goes in v4:
time: 111 us
  Pallas kernels  106 us (95%)
  between operations  3.68 us (3%)
  local copies, waits for them, and re-layouts  1.46 us (1%)
    pallas_call x1, Pallas kernels, per_device(): pl.pallas_call(kernel, out_shape=(jax.ShapeDtypeStruct((1, 1), F32), jax....  106 us

profile of v4, /device:TPU:1, one launch (start us, length us, event | category | flops | bytes accessed | tf_op | source)
XLA Modules:
  0.0 111.1 jit_solution(18355540205839064039)
XLA Ops:
  1.9 106.0 %pooled_loss.1 = (f32[1,1]{1,0:T(1,128)}, f32[8,1152]{1,0:T(8,128)}) custom-call(bf16[1024,1152]{1,0:T(8,128)(2,1)} %patches.1, s32[4]{0:T(128)} %counts.1, s32[4]{0:T(128)} %offsets.1, f32[1152]{0:T(1024)} %gain.1, bf16[36,4304]{1,0:T(8,128)(2,1)} %win_hbm.1, bf16[36,4304]{1,0:T(8,128)(2,1)} %bitcast.3, bf16[1152]{0:T(1024)(128)(2,1)} %probe.1, ...), custom_call_target="tpu_custom_call" | custom-call | flops 20308819968 | bytes 12582912 | tf_op jit(solution)/shard_map/pooled_loss/pallas_call | solution.py:689
  107.9 1.5 %fusion = (f32[4,1152]{1,0:T(4,128)}, f32[4,1152]{1,0:T(4,128)}) fusion(f32[8,1152]{1,0:T(8,128)} %get-tuple-element.6), kind=kLoop, calls=%fused_computation | loop fusion | bytes 73728 | tf_op jit(solution)/shard_map/slice | solution.py:760

commit v5 on v4

--- a/solution.py
+++ b/solution.py
@@ -32,13 +32,14 @@
 LAG_A, LAG_B, LAG_C, LAG_D, LAG_E = 3, 6, 9, 12, 13
 
 SHARED = 3
+SHARED_AT = (0, 3, 7)
 GATHERED = CHUNKS - SHARED
 TICKS = GATHERED + LAG_E
-HANDED_TICKS = (18, 21, 24)
-TWO_AT = (19, 22, 25)
+HANDED_TICKS = (17, 20, 23)
+TWO_AT = (18, 21, 24)
 TEXT_TICKS = (5, 9, 13, 17, 21, 24)
-PIECES = ((0, 4), (4, 10), (10, 17))
-PIECE_TICKS = (1, 4)
+PIECES = ((0, 4), (4, 8), (8, 17))
+PIECE_TICKS = (1, 2)
 
 Z, A_MINUS, A_PLUS, A_FAR, B_MINUS, B_PLUS, B_FAR, SIB, HAND = range(9)
 
@@ -235,7 +236,10 @@
     hand_to = tuple(jnp.where(k == 0, p, m) for p, m in zip(z_plus, z_minus))
 
     def gathered(i):
-        return jnp.where(i < SHARED, 2 * i + parity, i + SHARED)
+        c = i + 2 * SHARED - sum(jnp.where(i > at, 1, 0) for at in SHARED_AT)
+        for j, at in enumerate(SHARED_AT):
+            c = jnp.where(i == at, 2 * j + parity, c)
+        return c
 
     def part(c, p):
         pieces = [G[c, 0, p]]
@@ -264,11 +268,11 @@
             def _():
                 take_piece(p + 1)
 
-        for q in range(2):
-
-            @pl.when(2 * t + q < CHUNKS)
+        for q in range(4):
+
+            @pl.when(4 * t + q < CHUNKS)
             def _():
-                c = 2 * t + q
+                c = 4 * t + q
                 own = own_blocks.at[c]
 
                 @pl.when(jnp.logical_not(source))
@@ -326,7 +330,7 @@
             half = G.at[c, k]
             rcopy(half, half, g_ss.at[SIB, c], g_rs.at[SIB, c], sib).start()
 
-            @pl.when(i < SHARED)
+            @pl.when(sum(jnp.where(i == at, 1, 0) for at in SHARED_AT) == 1)
             def _():
                 rcopy(half, half, g_ss.at[HAND, c], g_rs.at[HAND, c], hand_to).start()
 
@@ -627,7 +631,7 @@
 
             @pl.when(c < SHARED)
             def _():
-                wait_send(G.at[e, k], g_ss.at[HAND, e])
+                wait_send(G.at[e, k], g_ss.at[HAND, 2 * c + parity])
 
         return carry
 

time: 111 us -> 110 us (level)
    pallas_call x1, Pallas kernels: 106 us -> 105 us  [per_device(): pl.pallas_call(kernel, out_shape=(jax.ShapeDtypeStruct((1, 1), F32), jax....]
where the time goes in v5:
time: 110 us
  Pallas kernels  105 us (95%)
  between operations  3.68 us (3%)
  local copies, waits for them, and re-layouts  1.46 us (1%)
    pallas_call x1, Pallas kernels, per_device(): pl.pallas_call(kernel, out_shape=(jax.ShapeDtypeStruct((1, 1), F32), jax....  105 us

profile of v5, /device:TPU:1, one launch (start us, length us, event | category | flops | bytes accessed | tf_op | source)
XLA Modules:
  0.0 109.7 jit_solution(10962497043607607266)
XLA Ops:
  1.9 104.6 %pooled_loss.1 = (f32[1,1]{1,0:T(1,128)}, f32[8,1152]{1,0:T(8,128)}) custom-call(bf16[1024,1152]{1,0:T(8,128)(2,1)} %patches.1, s32[4]{0:T(128)} %counts.1, s32[4]{0:T(128)} %offsets.1, f32[1152]{0:T(1024)} %gain.1, bf16[36,4304]{1,0:T(8,128)(2,1)} %win_hbm.1, bf16[36,4304]{1,0:T(8,128)(2,1)} %bitcast.3, bf16[1152]{0:T(1024)(128)(2,1)} %probe.1, ...), custom_call_target="tpu_custom_call" | custom-call | flops 20308819968 | bytes 12582912 | tf_op jit(solution)/shard_map/pooled_loss/pallas_call | solution.py:693
  106.5 1.5 %fusion = (f32[4,1152]{1,0:T(4,128)}, f32[4,1152]{1,0:T(4,128)}) fusion(f32[8,1152]{1,0:T(8,128)} %get-tuple-element.6), kind=kLoop, calls=%fused_computation | loop fusion | bytes 73728 | tf_op jit(solution)/shard_map/slice | solution.py:764

commit v6 on v5

--- a/solution.py
+++ b/solution.py
@@ -20,7 +20,7 @@
 PACK = 1024
 TEXTS = 1024
 SHARD = 36
-SLOT_ROWS = 48
+SLOT_ROWS = 36
 LANES = 128
 CHUNKS = 17
 HALF = CHUNKS * LANES
@@ -592,7 +592,7 @@
     push = jnp.dot(plane_slope, plane, preferred_element_type=F32)
     for zz in range(8):
         ps_s[zz] = push[8 * zz:8 * zz + 4, :]
-    for i in range(7):
+    for i in (3, 2, 4, 1, 5, 0, 6):
         to_z = m8(z + i + 1)
         rcopy(ps_s.at[to_z], ps_r.at[z], ps_ss.at[i], ps_rs.at[z], zs[i]).start()
     ps_r[z] = ps_s[z]

time: 110 us -> 110 us (level)
  no operation moved by 1% of the time
where the time goes in v6:
time: 110 us; the launch traced here: 109 us
  Pallas kernels  104 us (95%)
  between operations  3.68 us (3%)
  local copies, waits for them, and re-layouts  1.46 us (1%)
    pallas_call x1, Pallas kernels, per_device(): pl.pallas_call(kernel, out_shape=(jax.ShapeDtypeStruct((1, 1), F32), jax....  104 us

profile of v6, /device:TPU:1, one launch (start us, length us, event | category | flops | bytes accessed | tf_op | source)
XLA Modules:
  0.0 109.4 jit_solution(14949115960359186345)
XLA Ops:
  1.9 104.3 %pooled_loss.1 = (f32[1,1]{1,0:T(1,128)}, f32[8,1152]{1,0:T(8,128)}) custom-call(bf16[1024,1152]{1,0:T(8,128)(2,1)} %patches.1, s32[4]{0:T(128)} %counts.1, s32[4]{0:T(128)} %offsets.1, f32[1152]{0:T(1024)} %gain.1, bf16[36,4304]{1,0:T(8,128)(2,1)} %win_hbm.1, bf16[36,4304]{1,0:T(8,128)(2,1)} %bitcast.3, bf16[1152]{0:T(1024)(128)(2,1)} %probe.1, ...), custom_call_target="tpu_custom_call" | custom-call | flops 20308819968 | bytes 12582912 | tf_op jit(solution)/shard_map/pooled_loss/pallas_call | solution.py:693
  106.2 1.5 %fusion = (f32[4,1152]{1,0:T(4,128)}, f32[4,1152]{1,0:T(4,128)}) fusion(f32[8,1152]{1,0:T(8,128)} %get-tuple-element.6), kind=kLoop, calls=%fused_computation | loop fusion | bytes 73728 | tf_op jit(solution)/shard_map/slice | solution.py:764
